TPU v7x, 32 devices: a whole 2x2x4 slice. The times are simulated.
32 devices in a mesh: dp: 8 (over y, x, core), head: 4 (over z).
Axes of the slice: x: 2, y: 2, z: 4, core: 2. Of those that a mesh axis runs over, the one named last changes fastest.
Arguments:
- inputs: bfloat16 [16384, 768], P(('dp', 'head')), may hold values from -6 to 6
- seg_lengths: int32 [8, 8], P('dp'), may hold values from 0 to 1024, as said below
- ln1_gain: bfloat16 [768], replicated, may hold values from 0.5 to 1.5
- ln1_bias: bfloat16 [768], replicated, may hold values from -1.75 to 1.75
- qkv_weight: bfloat16 [768, 3, 768], P(None, None, 'head'), may hold values from -0.3125 to 0.3125
- qkv_bias: bfloat16 [3, 768], P(None, 'head'), may hold values from -1.75 to 1.75
- out_weight: bfloat16 [768, 768], P('head'), may hold values from -0.875 to 0.875
- out_bias: bfloat16 [768], replicated, may hold values from -1.75 to 1.75
- mem_mu: bfloat16 [12, 512], P('head'), may hold values from -0.25 to 0.25
- mem_sig: bfloat16 [12, 512], P('head'), may hold values from -0.25 to 0.25
- ln2_gain: bfloat16 [768], replicated, may hold values from 0.5 to 1.5
- ln2_bias: bfloat16 [768], replicated, may hold values from -1.75 to 1.75
- ff_in: bfloat16 [768, 3072], P(None, 'head'), may hold values from -0.21875 to 0.21875
- ff_in_bias: bfloat16 [3072], P('head'), may hold values from -1.75 to 1.75
- ff_out: bfloat16 [3072, 768], P('head'), may hold values from -0.109375 to 0.109375
- ff_out_bias: bfloat16 [768], replicated, may hold values from -1.75 to 1.75
- cotangent: bfloat16 [16384, 768], P(('dp', 'head')), may hold values from -6 to 6
Outputs:
- outputs: bfloat16 [16384, 768], P(('dp', 'head'))
- input_grad: bfloat16 [16384, 768], P(('dp', 'head'))
- ln1_gain_grad: float32 [768], replicated
- ln1_bias_grad: float32 [768], replicated
- qkv_weight_grad: float32 [768, 3, 768], P(None, None, 'head')
- qkv_bias_grad: float32 [3, 768], P(None, 'head')
- out_weight_grad: float32 [768, 768], P('head')
- out_bias_grad: float32 [768], replicated
- mem_mu_grad: float32 [12, 512], P('head')
- mem_sig_grad: float32 [12, 512], P('head')
- ln2_gain_grad: float32 [768], replicated
- ln2_bias_grad: float32 [768], replicated
- ff_in_grad: float32 [768, 3072], P(None, 'head')
- ff_in_bias_grad: float32 [3072], P('head')
- ff_out_grad: float32 [3072, 768], P('head')
- ff_out_bias_grad: float32 [768], replicated
Inputs may be any that keep to these rules, and one draw needn't show every extreme that they name: `seg_lengths`: each row lists one group's segments in order, four slots for each aligned run of 1024 tokens: lengths of 1, 2 or 4 times 256 that fill the run, then zeros; every group has a segment of 1024.
All inputs are finite; a program needn't handle non-finite values.
Results may differ from a plain program's by a relative error of at most 0.019.
The roundings to bfloat16 on the way count: a program that leaves them out, or rounds other values in their place, can miss the bound.
Values may be sent and summed in bfloat16 or wider, within the bound.
A program may use at most 256 MiB of HBM per device.

v0:
```python
import functools
import math

import jax
import jax.numpy as jnp
import ml_dtypes
import numpy as np
from jax import lax
from jax.experimental import pallas as pl
from jax.experimental.pallas import tpu as pltpu
from jax.sharding import PartitionSpec as P

HEAD_DIM = 64
BASIS = 512
UNIT = 256
LANES = 256
TAU = 0.75
RIDGE = 0.5
EPSILON = 1e-05
MESH = pl.DeviceIdType.MESH
SPREAD = 1.0 / 64.0
WIDTH = 1.0 / BASIS
LIVE = BASIS // 2
HIGHEST = lax.Precision.HIGHEST
F32 = jnp.float32
BF16 = jnp.bfloat16


def split_table(table):
    high = table.astype(np.float32).astype(ml_dtypes.bfloat16)
    low = (table.astype(np.float32) - high.astype(np.float32)).astype(ml_dtypes.bfloat16)
    return high, low


@functools.lru_cache(maxsize=None)
def basis_tables():
    centres = np.arange(BASIS) / (BASIS - 1)
    apart = centres[:, None] - centres[None, :]
    gram = np.exp(-apart * apart / (4.0 * WIDTH * WIDTH)) + RIDGE * np.eye(BASIS)
    solve = np.linalg.inv(gram)
    samples = (np.arange(BASIS) + 0.5) / BASIS
    near_gap = TAU * samples[:, None] - centres[None, :]
    far_gap = samples[:, None] - centres[None, :]
    near = np.exp(-near_gap * near_gap / (2.0 * WIDTH * WIDTH))
    far = np.exp(-far_gap * far_gap / (2.0 * WIDTH * WIDTH))
    contract = (near.T @ far) * (TAU / (BASIS * WIDTH * math.sqrt(math.pi)))
    joined = np.concatenate([solve @ contract, solve[:, LIVE:]], axis=1)
    high, low = split_table(joined)
    forward = np.concatenate([high, high, low], axis=1)
    backward = np.concatenate([high.T, high.T, low.T], axis=1)
    return forward, backward


def term_scale(units):
    return (1.0 - TAU) / (WIDTH * math.sqrt(math.pi) * UNIT) / units.astype(F32)


def split3(value):
    high = value.astype(BF16)
    low = (value - high.astype(F32)).astype(BF16)
    return jnp.concatenate([high, low, high], axis=0)


def dot(a, b, contract=((1,), (0,)), precision=None):
    return lax.dot_general(a, b, (contract, ((), ())), precision=precision, preferred_element_type=F32)


def head_rows(heads, width):
    row = lax.broadcasted_iota(jnp.int32, (8, width), 0)
    lane = lax.broadcasted_iota(jnp.int32, (8, width), 1) // HEAD_DIM
    return ((row == lane) | (row == lane + heads)) & (lane < heads)


def read_parts(logits, heads):
    location = 1.0 / (1.0 + jnp.exp(-logits))
    variance = (jnp.maximum(logits, 0.0) + jnp.log1p(jnp.exp(-jnp.abs(logits)))) * SPREAD + WIDTH * WIDTH
    return location[:heads], variance[heads : 2 * heads]


def place_of(index, length):
    return TAU + (1.0 - TAU) * (index.astype(F32) + 0.5) / (length.astype(F32) * UNIT)


def split_rows(value):
    high = value.astype(BF16)
    rest = value - high.astype(F32)
    mid = rest.astype(BF16)
    return high, mid, (rest - mid.astype(F32)).astype(BF16)


def three_pass(left, right_high, right_low, contract=((1,), (0,))):
    high = left.astype(BF16)
    low = (left - high.astype(F32)).astype(BF16)
    return dot(high, right_high, contract) + dot(low, right_high, contract) + dot(high, right_low, contract)


def advance_values(table, value):
    joined = BASIS + LIVE if table.shape[0] == BASIS else BASIS
    high, low = table[:BASIS, :BASIS], table[:BASIS, 2 * joined : 2 * joined + BASIS]
    value_high = value.astype(BF16)
    value_low = (value - value_high.astype(F32)).astype(BF16)
    return dot(high, value_high) + dot(high, value_low) + dot(low, value_high)


def segments_of(lengths, run, units):
    sizes = [lengths[0, run * units + s] // UNIT for s in range(units)]
    ends, total = [], 0
    for size in sizes:
        total = total + size
        ends.append(total)
    starts, spans, orders = [], [], []
    for b in range(units):
        start, span, order = 0, 0, 0
        for size, end in zip(sizes, ends):
            inside = (end > b) & (end - size <= b)
            start = start + jnp.where(inside, end - size, 0)
            span = span + jnp.where(inside, size, 0)
            order = order + jnp.where((end <= b) & (size > 0), 1, 0)
        starts.append(start)
        spans.append(span)
        orders.append(order)
    return starts, spans, orders


def other_of(index, distance):
    bit = 1
    while bit <= distance:
        if distance & bit:
            index = index + bit - 2 * bit * ((index // bit) % 2)
        bit *= 2
    return index


class Hops:
    def __init__(self, send, recv):
        self.send, self.recv, self.used = send, recv, 0

    def start(self, source, target, axis, bit):
        copy = pltpu.make_async_remote_copy(
            src_ref=source,
            dst_ref=target,
            send_sem=self.send.at[self.used],
            recv_sem=self.recv.at[self.used],
            device_id={axis: other_of(lax.axis_index(axis), bit)},
            device_id_type=MESH,
        )
        self.used += 1
        copy.start()
        return copy


def greet(neighbours):
    barrier = pltpu.get_barrier_semaphore()
    for axis, bit in neighbours:
        pl.semaphore_signal(
            barrier, inc=1, device_id={axis: other_of(lax.axis_index(axis), bit)}, device_id_type=MESH
        )
    pl.semaphore_wait(barrier, len(neighbours))


def set_out(pairs, sems, first):
    copies = [pltpu.make_async_copy(a, b, sems.at[first + k]) for k, (a, b) in enumerate(pairs)]
    for copy in copies:
        copy.start()
    return copies


def forward_kernel(
    heads, seg_lengths, source, packed, weight, out_weight, table, ff_in, ff_out,
    qkv_out, first_cols_out, flat_a_out, flat_b_out, logsum, values, probes, key_states, key_end, rows,
    mixed_0, mixed_1, mixed_2, mixed_3, in_bias, far_in, far_out, far_weight,
    qkv, first_rows, first_cols, flats, near, far, far_flat, small, far_row, bias_row, weight_mine, memory, sums, value_states, carried, value_ends, value_ins,
    projs, proj_ins, cols, discrete, mixed, mixed_in, send, recv, local_sems,
):
    own_rows, model = source.shape
    width = heads * HEAD_DIM
    units = qkv.shape[1]
    half = units // 2
    root = 1.0 / math.sqrt(HEAD_DIM)
    z = lax.axis_index("head")
    flip, run = (z % 2) * half, z // 2
    place = lax.axis_index("dp") % 8
    y, x, c = place // 4, (place // 2) % 2, place % 2
    slice_rows = model // 8
    at = lambda b: (b + flip) % units
    starts, lengths, orders = segments_of(seg_lengths, run, units)
    greet((("head", 1), ("head", 2), ("head", 3), ("dp", 1), ("dp", 2), ("dp", 4)))
    hops = Hops(send, recv)
    started = []

    def go(*args):
        started.append(hops.start(*args))
        return started[-1]

    part_rows, part_cols = far.shape[3:]
    mine = weight.at[
        pl.ds(pl.multiple_of((2 * y + x) * part_rows, 16), part_rows),
        pl.ds(pl.multiple_of(c * part_cols, 128), part_cols),
    ]
    small[...] = packed[0:16]
    bias_row[...] = jnp.broadcast_to(packed[22:23], bias_row.shape)
    narrow = width // 8
    chosen = jnp.zeros((narrow, model), F32)
    for j in range(8):
        chosen += jnp.where(place == j, out_weight[j * narrow : (j + 1) * narrow].astype(F32), 0.0)
    spare = jnp.zeros((weight_mine.shape[0] - narrow, model), F32)
    weight_mine[...] = jnp.concatenate([chosen, spare], axis=0).astype(BF16)
    slice_copy = go(mine, far.at[y, x, c], "head", 2)
    small_copy = go(small, far_row, "head", 2)
    row_copies = []
    for k in range(half):
        part = slice(k * UNIT, (k + 1) * UNIT)
        value = source[part].astype(F32)
        centred = value - jnp.mean(value, axis=-1, keepdims=True)
        factor = lax.rsqrt(jnp.mean(centred * centred, axis=-1, keepdims=True) + EPSILON)
        first_rows[part] = (centred * factor * packed[16:17] + packed[17:18]).astype(BF16)
        row_copies.append(go(first_rows.at[part], near.at[part], "head", 1))
    in_mine = ff_in.at[pl.ds(pl.multiple_of(place * slice_rows, 16), slice_rows)]
    out_mine = ff_out.at[pl.ds(pl.multiple_of(place * slice_rows, 16), slice_rows)]
    gathers = ((far_in, 2, 4), (far_weight, 2, 4), (far_out, 4, 2))
    stage = {}
    for r in (1, 2, 3):
        stage[r] = [
            go(in_mine, far_in.at[r - 1, y, x, c], "head", r),
            go(weight_mine, far_weight.at[r - 1, y, x, c], "head", r),
            go(out_mine, far_out.at[r - 1, y, x, c], "head", r),
        ]
    in_bias[0] = bias_row[...]
    bias_copies = [go(bias_row, in_bias.at[r], "head", r) for r in (1, 2, 3)]

    slice_copy.wait_recv()
    x_copy = go(far.at[y, x, c], far.at[y, x, c], "dp", 2)

    def widen(k, read):
        for i in range(3):
            flats[k, i * LANES : i * LANES + width] = read(slice(i * width, (i + 1) * width))
            flats[k, i * LANES + width : (i + 1) * LANES] = jnp.zeros((LANES - width, model), BF16)

    def project(k, unit, shift):
        span = slice(unit * UNIT, (unit + 1) * UNIT)
        qkv[k, unit] = (dot(first_rows[span], flats[k], ((1,), (1,))) + shift).astype(BF16)

    widen(0, lambda span: weight[span])
    for unit in range(half):
        project(0, unit, small[0:1])
    x_copy.wait_recv()
    y_copy = go(far.at[y, :, c], far.at[y, :, c], "dp", 4)
    first_cols[:, :own_rows] = first_rows[:own_rows].astype(F32).T.astype(BF16)
    y_copy.wait_recv()
    core_copy = go(far.at[:, :, c], far.at[:, :, c], "dp", 1)
    small_copy.wait_recv()
    for k, copy in enumerate(row_copies):
        copy.wait_recv()
        part = slice(k * UNIT, (k + 1) * UNIT)
        first_rows[own_rows + k * UNIT : own_rows + (k + 1) * UNIT] = near[part]
        project(0, half + k, small[0:1])

    def advance(r, step):
        for copy in stage[r]:
            copy.wait_recv()
        stage[r] = []
        for array, first, second in gathers:
            block = array.at[r - 1]
            if step == 1:
                part, bit = block.at[y, x, c], first
            elif step == 2:
                part, bit = (block.at[y, :, c] if first == 2 else block.at[:, x, c]), second
            else:
                part, bit = block.at[:, :, c], 1
            stage[r].append(go(part, part, "dp", bit))

    first_cols[:, own_rows:] = near[...].astype(F32).T.astype(BF16)
    core_copy.wait_recv()
    for i in range(8):
        row, col = (i // 2) * part_rows, (i % 2) * part_cols
        far_flat[row : row + part_rows, col : col + part_cols] = far[i // 4, (i // 2) % 2, i % 2]
    widen(1, lambda span: far_flat[span])
    for unit in range(units):
        project(1, unit, far_row[0:1])
    saved = set_out(
        [(qkv, qkv_out), (first_cols, first_cols_out), (flats.at[0], flat_a_out), (flats.at[1], flat_b_out)],
        local_sems, 0,
    )

    def probe_of(k):
        return jnp.where(k == 0, small[1:9, :BASIS], far_row[1:9, :BASIS])

    mask = head_rows(heads, LANES)

    def first_state(k, carry):
        memory[k] = jnp.zeros(memory.shape[1:], F32)
        row = probe_of(k)
        rows[k, 0:8] = row
        wide = 2 * (BASIS + LIVE)
        for i in range(1, 4):
            row = three_pass(row, table[:, :BASIS], table[:, wide : wide + BASIS])
            rows[k, 8 * i : 8 * i + 8] = row
        return carry

    lax.fori_loop(0, 2, first_state, 0)

    def state(b, k, carry):
        start, length = starts[b], lengths[b]
        now = memory[k]
        value_states[k, b] = now[:, LANES:]
        key_states[k, b] = now[:, :LANES].astype(BF16)
        if b > 0:
            probes[k, b] = jnp.where(mask, dot(rows[k, 0:8], now[:, :LANES], precision=HIGHEST), 0.0)
        else:
            probes[k, b] = jnp.zeros((8, LANES), F32)
        token = lax.broadcasted_iota(jnp.int32, (LIVE, UNIT), 1) + (b - start) * UNIT
        centre = (lax.broadcasted_iota(jnp.int32, (LIVE, UNIT), 0) + LIVE).astype(F32) / (BASIS - 1)
        gap = place_of(token, length) - centre
        psi = jnp.exp(gap * gap * (-0.5 / (WIDTH * WIDTH)))
        psi_high = psi.astype(BF16)
        psi_low = (psi - psi_high.astype(F32)).astype(BF16)
        pairs = qkv[k, at(b), :, LANES : 3 * LANES]
        fresh = dot(psi_high, pairs) + dot(psi_low, pairs)
        gathered = fresh if b == 0 else jnp.where(start == b, 0.0, sums[k]) + fresh
        sums[k] = gathered
        stacked = jnp.concatenate([now, gathered * term_scale(length)], axis=0)
        later = dot(table[...], split3(stacked))
        memory[k] = jnp.where(start + length == b + 1, later, now)
        return carry

    def end_state(k, carry):
        key = memory[k, :, :LANES]
        key_end[k] = key
        value_ends[k] = memory[k, :, LANES : LANES + width].astype(BF16)
        seen = dot(rows[k], key, precision=HIGHEST)
        for i in range(4):
            projs[k, 8 * i : 8 * i + 8] = jnp.where(mask, seen[8 * i : 8 * i + 8], 0.0)
        return carry

    def attend(b, k, carry):
        cols[k, b] = qkv[k, at(b), :, 2 * LANES : 3 * LANES].astype(F32).T.astype(BF16)
        query = qkv[k, at(b), :, 0:LANES].astype(F32) * root
        lane_head = lax.broadcasted_iota(jnp.int32, (UNIT, LANES), 1) // HEAD_DIM
        causal = lax.broadcasted_iota(jnp.int32, (UNIT, UNIT), 0) <= lax.broadcasted_iota(
            jnp.int32, (UNIT, UNIT), 1
        )
        away = [jnp.where(starts[b] <= j, 0.0, 1e30) for j in range(b)] + [0.0]
        for h in range(heads):
            own = jnp.where(lane_head == h, query, 0.0).astype(BF16)
            scores = [dot(qkv[k, at(j), :, LANES : 2 * LANES], own, ((1,), (1,))) for j in range(b + 1)]
            scores[b] = jnp.where(causal, scores[b], -1e30)
            highest = functools.reduce(
                jnp.maximum, [jnp.max(s, axis=0, keepdims=True) - away[j] for j, s in enumerate(scores)]
            )
            weights = [jnp.exp(s - (highest + away[j])) for j, s in enumerate(scores)]
            total = sum(jnp.sum(w, axis=0, keepdims=True) for w in weights)
            span = slice(h * HEAD_DIM, (h + 1) * HEAD_DIM)
            part = sum(dot(cols[k, j, span], weights[j].astype(BF16)) for j in range(b + 1))
            discrete[k, b, span] = part * (1.0 / total)
            logsum[k, b, h : h + 1] = highest + jnp.log(total)
        return carry

    def seen_value(k, carry):
        incoming = jnp.where(run > 0, value_ins[k].astype(F32), 0.0)
        carried[:, :width] = incoming
        carried[:, width:] = jnp.zeros((BASIS, LANES - width), F32)
        for b in range(units):
            if b > 0:
                carried[...] = jnp.where(starts[b] == b, advance_values(table, carried[...]), carried[...])
            values[k, b] = (value_states[k, b] + carried[...]).astype(BF16)
            gained = jnp.zeros((8, LANES), F32)
            for i in range(4):
                gained += jnp.where((orders[b] == i) & (run > 0), proj_ins[k, 8 * i : 8 * i + 8], 0.0)
            probes[k, b] = (probes[k, b] + gained) * root
        return carry

    def read(rel, k, carry):
        b = at(rel)
        query = qkv[k, rel, :, 0:LANES]
        logits = sum(dot(part, query, ((1,), (1,))) for part in split_rows(probes[k, b]))
        location, variance = read_parts(logits, heads)
        fall = -0.5 / variance
        peak = WIDTH * lax.rsqrt(variance)
        centres = lax.broadcasted_iota(jnp.int32, (BASIS, UNIT), 0).astype(F32) / (BASIS - 1)
        value_cols = values[k, b].astype(F32).T.astype(BF16)
        parts = []
        for h in range(heads):
            gap = centres - location[h : h + 1]
            density = jnp.exp(gap * gap * fall[h : h + 1]).astype(BF16)
            span = slice(h * HEAD_DIM, (h + 1) * HEAD_DIM)
            parts.append(discrete[k, b, span] + dot(value_cols[span], density) * peak[h : h + 1])
        mixed[k, rel] = jnp.concatenate(parts, axis=0).T.astype(BF16)
        return carry

    advance(1, 1)
    state_copies = []
    for k in range(2):
        for b in range(units):
            state(b, k, 0)
        end_state(k, 0)
        state_copies.append([
            go(value_ends.at[k], value_ins.at[1 - k], "head", 2), go(projs.at[k], proj_ins.at[1 - k], "head", 2)
        ])
        if k == 0:
            advance(2, 1)
            advance(1, 2)
    advance(3, 1)
    for b in range(units):
        lax.fori_loop(0, 2, functools.partial(attend, b), 0)
        if b == 0:
            advance(2, 2)
        if b == 2:
            advance(1, 3)
            advance(3, 2)
    mixed_copies = [None, None]
    for k in (1, 0):
        for copy in state_copies[1 - k]:
            copy.wait_recv()
        seen_value(k, 0)
        for rel in (2, 3, 0, 1):
            read(rel, k, 0)
            if rel == 3:
                mixed_copies[k] = go(mixed.at[k, half:], mixed_in.at[k], "head", 1)
        if k == 1:
            advance(2, 3)
    advance(3, 3)
    mixed_0[...] = mixed[0, :half].reshape(own_rows, width)
    mixed_2[...] = mixed[1, :half].reshape(own_rows, width)
    for copy in mixed_copies:
        copy.wait_recv()
    mixed_1[...] = mixed_in[0].reshape(own_rows, width)
    mixed_3[...] = mixed_in[1].reshape(own_rows, width)
    for copy in bias_copies + stage[1] + stage[2] + stage[3]:
        copy.wait_recv()
    for copy in started:
        copy.wait_send()
    for copy in saved:
        copy.wait()


def forward(seg_lengths, source, packed, weight, out_weight, ff_in, ff_out, heads):
    own_rows, model = source.shape
    units = 2 * own_rows // UNIT
    width = heads * HEAD_DIM
    hidden_part = ff_in.shape[1]
    rows = model // 8
    spaced = -(-width // 8 // 16) * 16
    table = jnp.asarray(basis_tables()[0])
    vmem, anywhere = pl.BlockSpec(memory_space=pltpu.VMEM), pl.BlockSpec(memory_space=pl.ANY)
    shape = jax.ShapeDtypeStruct
    hops = 2 + units // 2 + 3 + 3 * 3 * 4 + 3 + 4 + 2
    return pl.pallas_call(
        functools.partial(forward_kernel, heads),
        in_specs=[pl.BlockSpec(memory_space=pltpu.SMEM)] + [vmem] * 5 + [anywhere] * 2,
        out_specs=[anywhere] * 4 + [vmem] * 11 + [anywhere] * 3,
        out_shape=[
            shape((2, units, UNIT, 3 * LANES), BF16),
            shape((model, 2 * own_rows), BF16),
            shape((3 * LANES, model), BF16),
            shape((3 * LANES, model), BF16),
            shape((2, units, 8, UNIT), F32),
            shape((2, units, BASIS, LANES), BF16),
            shape((2, units, 8, LANES), F32),
            shape((2, units, BASIS, LANES), BF16),
            shape((2, BASIS, LANES), F32),
            shape((2, 32, BASIS), F32),
        ] + [shape((own_rows, width), BF16)] * 4 + [
            shape((4, 8, hidden_part), F32),
            shape((3, 2, 2, 2, rows, hidden_part), BF16),
            shape((3, 2, 2, 2, rows, model), BF16),
            shape((3, 2, 2, 2, spaced, model), BF16),
        ],
        scratch_shapes=[
            pltpu.VMEM((2, units, UNIT, 3 * LANES), BF16),
            pltpu.VMEM((2 * own_rows, model), BF16),
            pltpu.VMEM((model, 2 * own_rows), BF16),
            pltpu.VMEM((2, 3 * LANES, model), BF16),
            pltpu.VMEM((own_rows, model), BF16),
            pltpu.VMEM((2, 2, 2, 3 * width // 4, model // 2), BF16),
            pltpu.VMEM((3 * width, model), BF16),
            pltpu.VMEM((16, 3 * LANES), F32),
            pltpu.VMEM((16, 3 * LANES), F32),
            pltpu.VMEM((8, hidden_part), F32),
            pltpu.VMEM((spaced, model), BF16),
            pltpu.VMEM((2, BASIS, 2 * LANES), F32),
            pltpu.VMEM((2, LIVE, 2 * LANES), F32),
            pltpu.VMEM((2, units, BASIS, LANES), F32),
            pltpu.VMEM((BASIS, LANES), F32),
            pltpu.VMEM((2, BASIS, width), BF16),
            pltpu.VMEM((2, BASIS, width), BF16),
            pltpu.VMEM((2, 32, LANES), F32),
            pltpu.VMEM((2, 32, LANES), F32),
            pltpu.VMEM((2, units, LANES, UNIT), BF16),
            pltpu.VMEM((2, units, width, UNIT), F32),
            pltpu.VMEM((2, units, UNIT, width), BF16),
            pltpu.VMEM((2, units // 2, UNIT, width), BF16),
            pltpu.SemaphoreType.DMA((hops,)),
            pltpu.SemaphoreType.DMA((hops,)),
            pltpu.SemaphoreType.DMA((4,)),
        ],
        compiler_params=pltpu.CompilerParams(
            collective_id=1, has_side_effects=True, vmem_limit_bytes=60 << 20
        ),
        name="forward",
    )(seg_lengths, source, packed, weight, out_weight, table, ff_in, ff_out)


def whole(shape):
    return pl.BlockSpec(shape, lambda i: (0,) * len(shape))


def finish_kernel(given_in, given_out, given_weight, given_qkv, grad_in, grad_out, grad_weight, grad_qkv):
    step = pl.program_id(0)
    grad_in[...] = given_in[...].astype(F32)
    grad_out[...] = given_out[...].astype(F32)
    width = grad_qkv.shape[1]
    turned = given_qkv[...].astype(F32).T
    for i in range(3):

        @pl.when(step == i)
        def _():
            grad_qkv[0] = turned[i * width : (i + 1) * width]

    @pl.when(step == 0)
    def _():
        narrow = grad_weight.shape[0] // given_weight.shape[0]
        for j in range(given_weight.shape[0]):
            grad_weight[j * narrow : (j + 1) * narrow] = given_weight[j].astype(F32)[:narrow]


def finish(given_in, given_out, given_weight, given_qkv, width):
    model, columns = given_in.shape
    hidden_part = given_out.shape[0]
    return pl.pallas_call(
        finish_kernel,
        grid=(3,),
        in_specs=[
            pl.BlockSpec((model // 3, columns), lambda i: (i, 0)),
            pl.BlockSpec((hidden_part // 3, model), lambda i: (i, 0)),
            pl.BlockSpec(given_weight.shape, lambda i: (0, 0, 0)),
            pl.BlockSpec(given_qkv.shape, lambda i: (0, 0)),
        ],
        out_specs=[
            pl.BlockSpec((model // 3, columns), lambda i: (i, 0)),
            pl.BlockSpec((hidden_part // 3, model), lambda i: (i, 0)),
            pl.BlockSpec((width, model), lambda i: (0, 0)),
            pl.BlockSpec((1, width, model), lambda i: (i, 0, 0)),
        ],
        out_shape=[
            jax.ShapeDtypeStruct((model, columns), F32), jax.ShapeDtypeStruct((hidden_part, model), F32),
            jax.ShapeDtypeStruct((width, model), F32), jax.ShapeDtypeStruct((3, width, model), F32),
        ],
        compiler_params=pltpu.CompilerParams(vmem_limit_bytes=48 << 20),
        name="finish",
    )(given_in, given_out, given_weight, given_qkv)


def middle_kernel(
    source, cotangent, mixed_0, mixed_1, mixed_2, mixed_3, own_weight, far_weight, vectors, in_bias, own_in, own_out,
    far_in, far_out, outputs, grad_residual, grad_mixed_0, grad_mixed_1, grad_mixed_2, grad_mixed_3, grad_in, grad_out,
    grad_out_weight, sums, grad_in_bias,
    residual, inverse, second, second_cols, total, grad_second, in_now, out_now, out_weight,
):
    r = pl.program_id(0)
    slices, rows = own_in.shape[0], own_in.shape[1]
    model = source.shape[1]
    hidden_part = own_in.shape[2]
    out_bias, gain, shift, last_bias = (vectors[k : k + 1] for k in range(18, 22))

    @pl.when(r == 0)
    def _():
        value = source[...].astype(F32) + out_bias
        out_weight[0] = own_weight[...]
        narrow = own_weight.shape[0] // slices
        for k in range(far_weight.shape[0]):
            parts = [far_weight[k, j].astype(F32)[:narrow] for j in range(slices)]
            out_weight[k + 1] = jnp.concatenate(parts, axis=0).astype(BF16)
        for k, mixed in enumerate((mixed_0, mixed_1, mixed_2, mixed_3)):
            value += dot(mixed[...], out_weight[k])
        residual[...] = value
        centred = value - jnp.mean(value, axis=-1, keepdims=True)
        factor = lax.rsqrt(jnp.mean(centred * centred, axis=-1, keepdims=True) + EPSILON)
        inverse[...] = factor
        normal = centred * factor
        grad_residual[...] = normal
        rounded = (normal * gain + shift).astype(BF16)
        second[...] = rounded
        second_cols[...] = rounded.astype(F32).T.astype(BF16)
        total[...] = jnp.zeros_like(total)
        grad_second[...] = jnp.zeros_like(grad_second)
        grad_in_bias[...] = jnp.zeros_like(grad_in_bias)
        for j in range(slices):
            in_now[j * rows : (j + 1) * rows] = own_in[j]
            out_now[j * rows : (j + 1) * rows] = own_out[j]

    @pl.when(r > 0)
    def _():
        for j in range(slices):
            in_now[j * rows : (j + 1) * rows] = far_in[0, j]
            out_now[j * rows : (j + 1) * rows] = far_out[0, j]

    half = hidden_part // 2
    for t in range(2):
        span = slice(t * half, (t + 1) * half)
        hidden = dot(second[...], in_now[:, span]) + in_bias[r, 0:1, span]
        cube = hidden * hidden
        root = math.sqrt(2.0 / math.pi)
        bent = jnp.tanh(hidden * (root + (root * 0.044715) * cube))
        lifted = 0.5 + 0.5 * bent
        activation = (hidden * lifted).astype(BF16)
        slope = lifted + hidden * ((0.5 - 0.5 * bent * bent) * (root + (3.0 * root * 0.044715) * cube))
        total[...] += dot(activation, out_now[span])
        given = dot(cotangent[...], out_now[span], ((1,), (1,)))
        grad_hidden = (given * slope).astype(BF16)
        grad_second[...] += dot(grad_hidden, in_now[:, span], ((1,), (1,)))
        grad_in_bias[pl.ds(r, 1), span] = jnp.sum(grad_hidden.astype(F32), axis=0, keepdims=True)
        part = dot(activation, cotangent[...], ((0,), (0,))).astype(BF16)
        per = half // rows
        for k in range(per):
            grad_out[0, t * per + k] = part[k * rows : (k + 1) * rows]
        part = dot(second_cols[...], grad_hidden).astype(BF16)
        for j in range(slices):
            grad_in[0, j, :, span] = part[j * rows : (j + 1) * rows]

    @pl.when(r == pl.num_programs(0) - 1)
    def _():
        given = cotangent[...].astype(F32)
        outputs[...] = (residual[...] + total[...] + last_bias).astype(BF16)
        normal = grad_residual[...]
        grad = grad_second[...]
        scaled = grad * gain
        value = given + inverse[...] * (
            scaled
            - jnp.mean(scaled, axis=-1, keepdims=True)
            - normal * jnp.mean(scaled * normal, axis=-1, keepdims=True)
        )
        sums[0:1] = jnp.sum(value, axis=0, keepdims=True)
        sums[1:2] = jnp.sum(grad * normal, axis=0, keepdims=True)
        sums[2:3] = jnp.sum(grad, axis=0, keepdims=True)
        sums[3:4] = jnp.sum(given, axis=0, keepdims=True)
        sums[4:8] = jnp.zeros((4, model), F32)
        grad_residual[...] = value
        rounded = value.astype(BF16)
        grads = (grad_mixed_0, grad_mixed_1, grad_mixed_2, grad_mixed_3)
        for k, mixed in enumerate((mixed_0, mixed_1, mixed_2, mixed_3)):
            grads[k][...] = dot(rounded, out_weight[k], ((1,), (1,))).astype(BF16)
            product = dot(mixed[...], rounded, ((0,), (0,)))
            narrow = product.shape[0] // slices
            spare = jnp.zeros((grad_out_weight.shape[2] - narrow, model), F32)
            for j in range(slices):
                part = jnp.concatenate([product[j * narrow : (j + 1) * narrow], spare], axis=0)
                grad_out_weight[k, j] = part.astype(BF16)


def middle(source, cotangent, mixed, out_weight, far_weight, vectors, in_bias, own_in, own_out, far_in, far_out):
    own_rows, model = source.shape
    shards = far_in.shape[0] + 1
    slices, rows, hidden_part = own_in.shape
    narrow = mixed[0].shape
    far = pl.BlockSpec((1,) + own_in.shape, lambda r: (jnp.maximum(r - 1, 0), 0, 0, 0))
    part = pl.BlockSpec((1,) + own_in.shape, lambda r: (r, 0, 0, 0))
    macs = own_rows * model * (6 * shards * hidden_part + 3 * model)
    return pl.pallas_call(
        middle_kernel,
        grid_spec=pltpu.PrefetchScalarGridSpec(
            num_scalar_prefetch=0,
            grid=(shards,),
            in_specs=[whole(source.shape)] * 2 + [whole(narrow)] * 4 + [
                whole(out_weight.shape), whole(far_weight.shape), whole(vectors.shape), whole(in_bias.shape), whole(own_in.shape),
                whole(own_out.shape), far, far,
            ],
            out_specs=[whole(source.shape)] * 2 + [whole(narrow)] * 4 + [
                part, part, whole((shards,) + far_weight.shape[1:]), whole((8, model)), whole((shards, hidden_part))
            ],
            scratch_shapes=[
                pltpu.VMEM((own_rows, model), F32),
                pltpu.VMEM((own_rows, 1), F32),
                pltpu.VMEM((own_rows, model), BF16),
                pltpu.VMEM((model, own_rows), BF16),
                pltpu.VMEM((own_rows, model), F32),
                pltpu.VMEM((own_rows, model), F32),
                pltpu.VMEM((model, hidden_part), BF16),
                pltpu.VMEM((hidden_part, model), BF16),
                pltpu.VMEM((shards,) + narrow[1:] + (model,), BF16),
            ],
        ),
        out_shape=[
            jax.ShapeDtypeStruct(source.shape, BF16),
            jax.ShapeDtypeStruct(source.shape, F32),
        ] + [jax.ShapeDtypeStruct(narrow, BF16)] * 4 + [
            jax.ShapeDtypeStruct((shards, slices, rows, hidden_part), BF16),
            jax.ShapeDtypeStruct((shards, slices, rows, hidden_part), BF16),
            jax.ShapeDtypeStruct((shards,) + far_weight.shape[1:], BF16),
            jax.ShapeDtypeStruct((8, model), F32),
            jax.ShapeDtypeStruct((shards, hidden_part), F32),
        ],
        compiler_params=pltpu.CompilerParams(vmem_limit_bytes=60 << 20),
        cost_estimate=pl.CostEstimate(
            flops=2 * macs, bytes_accessed=30 << 20, transcendentals=own_rows * shards * hidden_part
        ),
        name="middle",
    )(source, cotangent, *mixed, out_weight, far_weight, vectors, in_bias, own_in, own_out, far_in, far_out)


def added(a, b):
    return (a.astype(F32) + b.astype(F32)).astype(BF16)


def backward_kernel(
    heads, seg_lengths, qkv, gm_0, gm_1, gm_2, gm_3, logsum, values, probes, key_states, key_end, rows, table,
    grad_in, grad_out, grad_weight, out, probe_grad, slice_in, slice_out, slice_weight,
    given, query_grad, memory_grad, row_grad, value_carried, value_back, value_in, row_back, row_in, carried, spread, key_grad, value_grad, cols,
    keep_in, keep_out, keep_weight, core_in, core_out, core_weight, one_in, one_out, one_weight,
    two_in, two_out, two_weight, z_in, z_out, z_weight, send, recv, local_sems,
):
    units = qkv.shape[1]
    half = units // 2
    width = heads * HEAD_DIM
    root = 1.0 / math.sqrt(HEAD_DIM)
    z = lax.axis_index("head")
    flip, run = (z % 2) * half, z // 2
    place = lax.axis_index("dp") % 8
    y, x, c = place // 4, (place // 2) % 2, place % 2
    at = lambda b: (b + flip) % units
    starts, lengths, orders = segments_of(seg_lengths, run, units)
    greet((("head", 1), ("head", 2), ("head", 3), ("dp", 1), ("dp", 2), ("dp", 4)))
    hops = Hops(send, recv)
    started = []

    def go(*args):
        started.append(hops.start(*args))
        return started[-1]

    given_copies = [go(gm_1, given.at[0, half:], "head", 1), go(gm_3, given.at[1, half:], "head", 1)]
    sums = (
        (grad_in, keep_in, core_in, one_in, two_in, z_in, True),
        (grad_weight, keep_weight, core_weight, one_weight, two_weight, z_weight, True),
        (grad_out, keep_out, core_out, one_out, two_out, z_out, False),
    )
    stage, local_copies = {}, {}
    for i, r in enumerate((2, 1, 3, 0)):
        stage[r], local_copies[r] = [], []
        for n, (term, keep, core, _, _, _, _) in enumerate(sums):
            stage[r].append(go(term.at[r, :, :, 1 - c], core.at[r], "dp", 1))
            copy = pltpu.make_async_copy(term.at[r, :, :, c], keep.at[r], local_sems.at[3 * i + n])
            copy.start()
            local_copies[r].append(copy)

    def first_hop(r):
        for n, (_, keep, core, one, _, _, along_x) in enumerate(sums):
            local_copies[r][n].wait()
            stage[r][n].wait_recv()
            keep[r] = added(keep[r], core[r])
            part = keep.at[r, :, 1 - x] if along_x else keep.at[r, 1 - y]
            stage[r][n] = go(part, one.at[r], "dp", 2 if along_x else 4)

    def second_hop(r):
        for n, (_, keep, _, one, two, _, along_x) in enumerate(sums):
            stage[r][n].wait_recv()
            kept = keep[r, :, x] if along_x else keep[r, y]
            one[r] = added(kept, one[r])
            part = one.at[r, 1 - y] if along_x else one.at[r, 1 - x]
            stage[r][n] = go(part, two.at[r], "dp", 4 if along_x else 2)

    def third_hop(r):
        for n, (_, _, _, one, two, far, along_x) in enumerate(sums):
            stage[r][n].wait_recv()
            kept = one[r, y] if along_x else one[r, x]
            two[r] = added(kept, two[r])
            if r:
                stage[r][n] = go(two.at[r], far.at[r - 1], "head", r)

    for k, own in enumerate((gm_0, gm_2)):
        given[k, :half] = own[...]
    mask = head_rows(heads, LANES)
    lane_head = lax.broadcasted_iota(jnp.int32, (UNIT, LANES), 1) // HEAD_DIM

    def given_of(k, b):
        return jnp.concatenate([given[k, at(b)], jnp.zeros((UNIT, LANES - width), BF16)], axis=1).astype(F32)

    def read_back(rel, k, carry):
        b = at(rel)
        query = qkv[k, rel, :, 0:LANES]
        full = given_of(k, b)
        probe = probes[k, b]
        logits = sum(dot(part, query, ((1,), (1,))) for part in split_rows(probe))
        location, variance = read_parts(logits, heads)
        inverse = 1.0 / variance
        fall = -0.5 * inverse
        peak = WIDTH * lax.rsqrt(variance)
        centres = lax.broadcasted_iota(jnp.int32, (BASIS, UNIT), 0).astype(F32) / (BASIS - 1)
        along, across = [], []
        total = jnp.zeros((BASIS, LANES), F32)
        for h in range(heads):
            own_given = jnp.where(lane_head == h, full, 0.0).astype(BF16)
            gap = centres - location[h : h + 1]
            square = gap * gap
            density = jnp.exp(square * fall[h : h + 1]) * peak[h : h + 1]
            grad_density = dot(values[k, b], own_given, ((1,), (1,)))
            total += dot(density.astype(BF16), own_given)
            weighed = density * grad_density
            moment = weighed * gap
            zeroth = jnp.sum(weighed, axis=0, keepdims=True)
            first = jnp.sum(moment, axis=0, keepdims=True)
            second = jnp.sum(moment * gap, axis=0, keepdims=True)
            along.append(first * inverse[h : h + 1])
            across.append(0.5 * inverse[h : h + 1] * (second * inverse[h : h + 1] - zeroth))
        sigmoid = 1.0 / (1.0 + jnp.exp(-logits))
        grad_location = jnp.concatenate(along, axis=0) * location * (1.0 - location)
        grad_variance = jnp.concatenate(across, axis=0) * SPREAD * sigmoid[heads : 2 * heads]
        grad_logits = jnp.concatenate(
            [grad_location, grad_variance, jnp.zeros((8 - 2 * heads, UNIT), F32)], axis=0
        )
        padded = jnp.concatenate([grad_logits, jnp.zeros((120, UNIT), F32)], axis=0)
        probe_cols = jnp.concatenate([probe, jnp.zeros((120, LANES), F32)], axis=0).T
        query_grad[k, b] = dot(probe_cols, padded, precision=HIGHEST)[:width]
        fresh = jnp.where(mask, dot(grad_logits, query.astype(F32), precision=HIGHEST), 0.0) * root
        memory_grad[k, b] = total
        row_grad[k, b] = fresh
        return carry

    def gather_back(k, carry):
        probe = jnp.zeros((8, BASIS), F32)
        for i in range(4):
            row_back[k, 8 * i : 8 * i + 8] = jnp.zeros((8, LANES), F32)
        for b in range(units - 1, -1, -1):
            fresh, total = row_grad[k, b], memory_grad[k, b]
            probe += dot(fresh, key_states[k, b].astype(F32), ((1,), (1,)), HIGHEST)
            for i in range(4):
                row_back[k, 8 * i : 8 * i + 8] += jnp.where(orders[b] == i, fresh, 0.0)
            if b < units - 1:
                ends = starts[b] + lengths[b] == b + 1
                total = jnp.where(ends, 0.0, memory_grad[k, b + 1]) + total
                memory_grad[k, b] = total
                row_grad[k, b] = jnp.where(ends, 0.0, row_grad[k, b + 1]) + fresh
            before = jnp.zeros((BASIS, LANES), F32) if b == units - 1 else value_carried[k]
            if b > 0:
                value_carried[k] = jnp.where(starts[b] == b, advance_values(table, before + total), before)
            else:
                value_back[k] = (before + total)[:, :width].astype(BF16)
        probe_grad[k] = probe
        return carry

    def attend_back(b, k, carry):
        query = qkv[k, at(b), :, 0:LANES].astype(F32) * root
        full = given_of(k, b)
        causal = lax.broadcasted_iota(jnp.int32, (UNIT, UNIT), 0) <= lax.broadcasted_iota(
            jnp.int32, (UNIT, UNIT), 1
        )
        away = [jnp.where(starts[b] <= j, 0.0, 1e30) for j in range(b)] + [0.0]
        owns = [jnp.where(lane_head == h, query, 0.0).astype(BF16) for h in range(heads)]
        own_givens = [jnp.where(lane_head == h, full, 0.0).astype(BF16) for h in range(heads)]
        grads, probs = [], []
        for h in range(heads):
            prob_h, product_h = [], []
            inner = jnp.zeros((1, UNIT), F32)
            for j in range(b + 1):
                score = dot(qkv[k, at(j), :, LANES : 2 * LANES], owns[h], ((1,), (1,)))
                if j == b:
                    score = jnp.where(causal, score, -1e30)
                prob = jnp.exp(score - (logsum[k, b, h : h + 1] + away[j]))
                product = prob * dot(qkv[k, at(j), :, 2 * LANES : 3 * LANES], own_givens[h], ((1,), (1,)))
                inner += jnp.sum(product, axis=0, keepdims=True)
                prob_h.append(prob)
                product_h.append(product)
            span = slice(h * HEAD_DIM, (h + 1) * HEAD_DIM)
            grad_h = [(product_h[j] - prob_h[j] * inner).astype(BF16) for j in range(b + 1)]
            result = sum(dot(cols[k, j, span], grad_h[j]) for j in range(b + 1))
            query_grad[k, b, span] = query_grad[k, b, span] + result * root
            grads.append(grad_h)
            probs.append([prob.astype(BF16) for prob in prob_h])
        own_all = jnp.concatenate(owns, axis=0)
        given_all = jnp.concatenate(own_givens, axis=0)
        for j in range(b + 1):
            keys = dot(jnp.concatenate([grads[h][j] for h in range(heads)], axis=1), own_all)
            vals = dot(jnp.concatenate([probs[h][j] for h in range(heads)], axis=1), given_all)
            if b == units - 1:
                key_grad[k, j], value_grad[k, j] = keys, vals
            else:
                key_grad[k, j] += keys
                value_grad[k, j] += vals
        return carry

    def carry_back(k, total, units_before):
        moved = dot(table[...], split3(total))
        return moved[:BASIS], (moved[BASIS:] * term_scale(units_before)).astype(BF16)

    def end_back(k, carry):
        row = jnp.where(run == 0, row_in[k], 0.0)
        value = jnp.where(run == 0, value_in[k].astype(F32), 0.0)
        grad_keys = dot(rows[k], row, ((0,), (0,)), HIGHEST)
        total = jnp.concatenate([grad_keys, value, jnp.zeros((BASIS, LANES - width), F32)], axis=1)
        carried[k], spread[k] = carry_back(k, total, lengths[units - 1])
        seen = dot(row, key_end[k], ((1,), (1,)), HIGHEST)
        gained = seen[24:32]
        for i in (2, 1, 0):
            gained = three_pass(gained, table[:BASIS, :BASIS], table[:BASIS, 2 * BASIS : 3 * BASIS])
            gained = gained + seen[8 * i : 8 * i + 8]
        probe_grad[k] += gained
        return carry

    def finish(b, k, carry):
        start, length = starts[b], lengths[b]
        token = lax.broadcasted_iota(jnp.int32, (UNIT, LIVE), 0) + (b - start) * UNIT
        centre = (lax.broadcasted_iota(jnp.int32, (UNIT, LIVE), 1) + LIVE).astype(F32) / (BASIS - 1)
        gap = place_of(token, length) - centre
        psi = jnp.exp(gap * gap * (-0.5 / (WIDTH * WIDTH))).astype(BF16)
        pair_grad = dot(psi, spread[k])
        query_rows = query_grad[k, b].T.astype(BF16)
        out[k, at(b), :, :LANES] = jnp.concatenate([query_rows, jnp.zeros((UNIT, LANES - width), BF16)], axis=1)
        out[k, at(b), :, LANES : 2 * LANES] = (key_grad[k, b] + pair_grad[:, :LANES]).astype(BF16)
        out[k, at(b), :, 2 * LANES :] = (value_grad[k, b] + pair_grad[:, LANES:]).astype(BF16)
        if b > 0:
            grad_keys = dot(rows[k, 0:8], row_grad[k, b], ((0,), (0,)), HIGHEST)
            total = carried[k] + jnp.concatenate([grad_keys, memory_grad[k, b]], axis=1)
            moved, spread_now = carry_back(k, total, lengths[b - 1])
            carried[k] = jnp.where(start == b, moved, carried[k])
            spread[k] = jnp.where(start == b, spread_now.astype(F32), spread[k].astype(F32)).astype(BF16)
        return carry

    def both(step, *args):
        lax.fori_loop(0, 2, functools.partial(step, *args), 0)

    def turn(k, carry):
        for b in range(units):
            cols[k, b] = qkv[k, at(b), :, LANES : 2 * LANES].astype(F32).T.astype(BF16)
        return carry

    lax.fori_loop(0, 2, turn, 0)
    both(read_back, 0)
    first_hop(2)
    both(read_back, 1)
    first_hop(1)
    for copy in given_copies:
        copy.wait_recv()
    both(read_back, 2)
    first_hop(3)
    first_hop(0)
    both(read_back, 3)
    second_hop(2)
    back_copies = []
    for k in range(2):
        gather_back(k, 0)
        back_copies += [
            go(value_back.at[k], value_in.at[1 - k], "head", 2), go(row_back.at[k], row_in.at[1 - k], "head", 2)
        ]
    second_hop(1)
    both(attend_back, 3)
    second_hop(3)
    second_hop(0)
    third_hop(2)
    both(attend_back, 2)
    third_hop(1)
    third_hop(3)
    both(attend_back, 1)
    third_hop(0)
    both(attend_back, 0)
    for copy in back_copies:
        copy.wait_recv()
    lax.fori_loop(0, 2, end_back, 0)
    for b in range(units - 1, -1, -1):
        both(finish, b)
    for n, (_, _, _, _, two, far, _) in enumerate(sums):
        total = two[0].astype(F32)
        for r in (1, 2, 3):
            stage[r][n].wait_recv()
            total += far[r - 1].astype(F32)
        (slice_in, slice_weight, slice_out)[n][...] = total.astype(BF16)
    for copy in started:
        copy.wait_send()


def backward(seg_lengths, qkv, grad_mixed, logsum, values, probes, key_states, key_end, rows, grad_in, grad_out, grad_weight, heads):
    units = qkv.shape[1]
    width = heads * HEAD_DIM
    table = jnp.asarray(basis_tables()[1])
    vmem, anywhere = pl.BlockSpec(memory_space=pltpu.VMEM), pl.BlockSpec(memory_space=pl.ANY)
    shape = jax.ShapeDtypeStruct
    slices = [grad_in.shape[4:], grad_out.shape[4:], grad_weight.shape[4:]]
    hops = 2 + 3 * 4 * 3 + 3 * 3 + 4
    return pl.pallas_call(
        functools.partial(backward_kernel, heads),
        in_specs=[pl.BlockSpec(memory_space=pltpu.SMEM)] + [vmem] * 12 + [anywhere] * 3,
        out_specs=[vmem] * 5,
        out_shape=[shape(qkv.shape, BF16), shape((2, 8, BASIS), F32)] + [shape(part, BF16) for part in slices],
        scratch_shapes=[
            pltpu.VMEM((2, units, UNIT, width), BF16),
            pltpu.VMEM((2, units, width, UNIT), F32),
            pltpu.VMEM((2, units, BASIS, LANES), F32),
            pltpu.VMEM((2, units, 8, LANES), F32),
            pltpu.VMEM((2, BASIS, LANES), F32),
            pltpu.VMEM((2, BASIS, width), BF16),
            pltpu.VMEM((2, BASIS, width), BF16),
            pltpu.VMEM((2, 32, LANES), F32),
            pltpu.VMEM((2, 32, LANES), F32),
            pltpu.VMEM((2, BASIS, 2 * LANES), F32),
            pltpu.VMEM((2, LIVE, 2 * LANES), BF16),
            pltpu.VMEM((2, units, UNIT, LANES), F32),
            pltpu.VMEM((2, units, UNIT, LANES), F32),
            pltpu.VMEM((2, units, LANES, UNIT), BF16),
        ]
        + [pltpu.VMEM((4, 2, 2) + part, BF16) for part in slices]
        + [pltpu.VMEM((4, 2, 2) + part, BF16) for part in slices]
        + [pltpu.VMEM((4, 2) + part, BF16) for part in slices]
        + [pltpu.VMEM((4,) + part, BF16) for part in slices]
        + [pltpu.VMEM((3,) + part, BF16) for part in slices]
        + [
            pltpu.SemaphoreType.DMA((hops,)),
            pltpu.SemaphoreType.DMA((hops,)),
            pltpu.SemaphoreType.DMA((12,)),
        ],
        compiler_params=pltpu.CompilerParams(
            collective_id=2, has_side_effects=True, vmem_limit_bytes=62 << 20
        ),
        name="backward",
    )(
        seg_lengths, qkv, *grad_mixed, logsum, values, probes, key_states, key_end, rows, table, grad_in, grad_out, grad_weight
    )


def tail_kernel(
    heads, outer, grads, first_cols, flat_a, flat_b, grad_residual, source, packed, slice_in, slice_out, slice_weight,
    sums, in_bias_part, probe_grad, input_grad, whole_in, whole_out, whole_weight, whole_qkv, shared_out, owned_out,
    row_grad, near, kept, part_a, part_b, core_a, core_b, one_a, one_b, two_a, two_b, far_b, total, outer_in,
    gather_in, gather_out, gather_weight, gather_qkv,
    shared, shared_in, block, block_in, bias_block, bias_in, joined, joined_in, send, recv,
):
    own_rows, model = source.shape
    units = grads.shape[1]
    half = units // 2
    width = heads * HEAD_DIM
    z = lax.axis_index("head")
    place = lax.axis_index("dp") % 8
    y, x, c = place // 4, (place // 2) % 2, place % 2
    rows = model // 8
    greet(
        (("head", 1), ("head", 2), ("head", 3), ("dp", 1), ("dp", 2), ("dp", 4)) + tuple(("dp", bit) for bit in outer)
    )
    hops = Hops(send, recv)
    started = []

    def go(*args):
        started.append(hops.start(*args))
        return started[-1]

    def row_of(rel):
        return dot(grads[0, rel], flat_a[...]) + dot(grads[1, rel], flat_b[...])

    row_copies = []
    for k in range(half):
        row_grad[k] = row_of(half + k).astype(BF16)
        row_copies.append(go(row_grad.at[k], near.at[k], "head", 1))

    gathers = ((slice_in, gather_in, True), (slice_weight, gather_weight, True), (slice_out, gather_out, False))
    for own, gather, _ in gathers:
        gather[y, x, c] = own[...]

    def spread_first(gather, along_x):
        part = gather.at[y, x, c]
        return go(part, part, "dp", 2 if along_x else 4)

    def spread_second(gather, along_x):
        part = gather.at[y, :, c] if along_x else gather.at[:, x, c]
        return go(part, part, "dp", 4 if along_x else 2)

    def spread_third(gather):
        part = gather.at[:, :, c]
        return go(part, part, "dp", 1)

    core_copies = []
    for k, part, core in ((1, part_b, core_b), (0, part_a, core_a)):
        product = dot(first_cols[...], grads[k].reshape(2 * own_rows, 3 * LANES))
        product = jnp.concatenate([product[:, i * LANES : i * LANES + width] for i in range(3)], axis=1).astype(BF16)
        for j in range(8):
            part[j // 4, (j // 2) % 2, j % 2] = product[j * rows : (j + 1) * rows]
        core_copies.append(go(part.at[:, :, 1 - c], core, "dp", 1))
    spreads = [spread_first(gather, along_x) for _, gather, along_x in gathers]
    for k in range(half):
        kept[k] = row_of(k)

    core_copies[0].wait_recv()
    core_b[...] = added(part_b[:, :, c], core_b[...])
    one_copy_b = go(core_b.at[1 - y], one_b, "dp", 4)
    core_copies[1].wait_recv()
    core_a[...] = added(part_a[:, :, c], core_a[...])
    one_copy_a = go(core_a.at[:, 1 - x], one_a, "dp", 2)

    bias_a = jnp.sum(grads[0].reshape(2 * own_rows, 3 * LANES).astype(F32), axis=0, keepdims=True)
    bias_b = jnp.sum(grads[1].reshape(2 * own_rows, 3 * LANES).astype(F32), axis=0, keepdims=True)
    edge = jnp.zeros((8, model - BASIS), F32)
    fill = jnp.zeros((6, model), F32)
    for k, bias in ((0, bias_a), (1, bias_b)):
        block[k, 0:8] = jnp.concatenate([probe_grad[k], edge], axis=1)
        block[k, 8:16] = jnp.concatenate([bias, in_bias_part[2 * k : 2 * k + 1], fill], axis=0)
        bias_block[k] = jnp.concatenate([in_bias_part[2 * k + 1 : 2 * k + 2], jnp.zeros((7, model), F32)], axis=0)
    block_copy = go(block.at[1], block_in, "head", 2)
    bias_copies = [go(bias_block.at[0], bias_in.at[0], "head", 1), go(bias_block.at[1], bias_in.at[1], "head", 3)]

    value = source[...].astype(F32)
    centred = value - jnp.mean(value, axis=-1, keepdims=True)
    factor = lax.rsqrt(jnp.mean(centred * centred, axis=-1, keepdims=True) + EPSILON)
    normal = centred * factor

    one_copy_b.wait_recv()
    one_b[...] = added(core_b[y], one_b[...])
    two_copy_b = go(one_b.at[1 - x], two_b, "dp", 2)
    one_copy_a.wait_recv()
    one_a[...] = added(core_a[:, x], one_a[...])
    two_copy_a = go(one_a.at[1 - y], two_a, "dp", 4)
    for copy in row_copies:
        copy.wait_recv()
    two_copy_b.wait_recv()
    two_b[...] = added(one_b[x], two_b[...])
    far_copy = go(two_b, far_b, "head", 2)

    grad = kept[...].reshape(own_rows, model) + near[...].reshape(own_rows, model).astype(F32)
    scaled = grad * packed[16:17]
    change = factor * (
        scaled
        - jnp.mean(scaled, axis=-1, keepdims=True)
        - normal * jnp.mean(scaled * normal, axis=-1, keepdims=True)
    )
    input_grad[...] = (grad_residual[...] + change).astype(BF16)
    shared[...] = jnp.concatenate(
        [jnp.sum(grad * normal, axis=0, keepdims=True), jnp.sum(grad, axis=0, keepdims=True), sums[0:6]], axis=0
    )
    shared_copies = [go(shared, shared_in.at[r - 1], "head", r) for r in (1, 2, 3)]
    spreads = [copy.wait_recv() or spread_second(gather, along_x) for copy, (_, gather, along_x) in zip(spreads, gathers)]

    two_copy_a.wait_recv()
    own_sum = added(one_a[y], two_a[...]).astype(F32)
    far_copy.wait_recv()
    total[0] = (own_sum + far_b[...].astype(F32)).astype(BF16)
    for n, bit in enumerate(outer):
        copy = go(total.at[n], outer_in.at[n], "dp", bit)
        copy.wait_recv()
        total[n + 1] = added(total[n], outer_in[n])
    gather_qkv[y, x, c] = total[len(outer)]
    cut = rows // 2
    upper, lower = pl.ds(0, cut), pl.ds(cut, cut)
    qkv_parts = [gather_qkv.at[y, x, c, upper], gather_qkv.at[y, x, c, lower]]
    qkv_copies = [go(qkv_parts[0], qkv_parts[0], "dp", 2), go(qkv_parts[1], qkv_parts[1], "dp", 4)]

    block_copy.wait_recv()
    for copy in bias_copies + shared_copies:
        copy.wait_recv()
    owned = block[0] + block_in[...]
    bias_rows = bias_in[0] + bias_in[1]
    owned_rows = jnp.concatenate([owned[8:9], owned[9:10] + bias_rows[0:1], owned[10:16]], axis=0)
    joined[0] = jnp.concatenate(
        [shared[...] + shared_in[0] + shared_in[1] + shared_in[2], owned[0:8], owned_rows], axis=0
    )
    spreads = [copy.wait_recv() or spread_third(gather) for copy, (_, gather, _) in zip(spreads, gathers)]
    for n, bit in enumerate((2, 4, 1) + outer):
        copy = go(joined.at[n], joined_in.at[n], "dp", bit)
        if n == 1:
            for copy_one in qkv_copies:
                copy_one.wait_recv()
            qkv_parts = [gather_qkv.at[y, :, c, upper], gather_qkv.at[:, x, c, lower]]
            qkv_copies = [go(qkv_parts[0], qkv_parts[0], "dp", 4), go(qkv_parts[1], qkv_parts[1], "dp", 2)]
        copy.wait_recv()
        joined[n + 1] = joined[n] + joined_in[n]
    last = joined[3 + len(outer)]
    shared_out[...] = last[0:8]
    owned_out[...] = last[8:24]
    for copy, (_, gather, _), out in zip(spreads, gathers, (whole_in, whole_weight, whole_out)):
        copy.wait_recv()
        out[...] = gather[...]
    for copy in qkv_copies:
        copy.wait_recv()
    spread_third(gather_qkv).wait_recv()
    whole_qkv[...] = gather_qkv[...]
    for copy in started:
        copy.wait_send()


def tail(grads, first_cols, flat_a, flat_b, grad_residual, source, packed, slices, sums, in_bias_part, probe_grad, outer, heads):
    own_rows, model = source.shape
    units = grads.shape[1]
    rows = model // 8
    vmem = pl.BlockSpec(memory_space=pltpu.VMEM)
    shape = jax.ShapeDtypeStruct
    slice_in, slice_out, slice_weight = slices
    plane = lambda part: (2, 2, 2) + part
    part = (rows, 3 * heads * HEAD_DIM)
    hops = units // 2 + 9 + 2 + 2 + 2 + 1 + 5 + 1 + 2 + 3 + 3 + 2 * len(outer)
    return pl.pallas_call(
        functools.partial(tail_kernel, heads, outer),
        in_specs=[vmem] * 13,
        out_specs=[vmem] * 7,
        out_shape=[
            shape(source.shape, BF16), shape(plane(slice_in.shape), BF16), shape(plane(slice_out.shape), BF16),
            shape(plane(slice_weight.shape), BF16), shape(plane(part), BF16), shape((8, model), F32),
            shape((16, model), F32),
        ],
        scratch_shapes=[
            pltpu.VMEM((units // 2, UNIT, model), BF16),
            pltpu.VMEM((units // 2, UNIT, model), BF16),
            pltpu.VMEM((units // 2, UNIT, model), F32),
            pltpu.VMEM(plane(part), BF16),
            pltpu.VMEM(plane(part), BF16),
            pltpu.VMEM((2, 2) + part, BF16),
            pltpu.VMEM((2, 2) + part, BF16),
            pltpu.VMEM((2,) + part, BF16),
            pltpu.VMEM((2,) + part, BF16),
            pltpu.VMEM(part, BF16),
            pltpu.VMEM(part, BF16),
            pltpu.VMEM(part, BF16),
            pltpu.VMEM((1 + len(outer),) + part, BF16),
            pltpu.VMEM((max(1, len(outer)),) + part, BF16),
            pltpu.VMEM(plane(slice_in.shape), BF16),
            pltpu.VMEM(plane(slice_out.shape), BF16),
            pltpu.VMEM(plane(slice_weight.shape), BF16),
            pltpu.VMEM(plane(part), BF16),
            pltpu.VMEM((8, model), F32),
            pltpu.VMEM((3, 8, model), F32),
            pltpu.VMEM((2, 16, model), F32),
            pltpu.VMEM((16, model), F32),
            pltpu.VMEM((2, 8, model), F32),
            pltpu.VMEM((2, 8, model), F32),
            pltpu.VMEM((4 + len(outer), 24, model), F32),
            pltpu.VMEM((3 + len(outer), 24, model), F32),
            pltpu.SemaphoreType.DMA((hops,)),
            pltpu.SemaphoreType.DMA((hops,)),
        ],
        compiler_params=pltpu.CompilerParams(
            collective_id=3, has_side_effects=True, vmem_limit_bytes=60 << 20
        ),
        name="tail",
    )(
        grads, first_cols, flat_a, flat_b, grad_residual, source, packed, slice_in, slice_out, slice_weight, sums,
        in_bias_part, probe_grad,
    )


def exchange(value, axis, bit):
    size = lax.axis_size(axis)
    return lax.ppermute(value, axis, [(j, j ^ bit) for j in range(size)])


def local(
    inputs, seg_lengths, ln1_gain, ln1_bias, qkv_weight, qkv_bias, out_weight, out_bias, mem_mu, mem_sig,
    ln2_gain, ln2_bias, ff_in, ff_in_bias, ff_out, ff_out_bias, cotangent,
):
    own_rows, model = inputs.shape
    shards = lax.axis_size("head")
    members = lax.axis_size("dp")
    width = qkv_weight.shape[2]
    heads = width // HEAD_DIM
    hidden_part = ff_in.shape[1]
    units = 2 * own_rows // UNIT
    slices = 8
    outer = tuple(1 << k for k in range(3, 16) if 1 << k < members)
    rows = model // slices

    bias_row = jnp.pad(qkv_bias, ((0, 0), (0, LANES - width))).reshape(1, 3 * LANES)
    edge = 3 * LANES - BASIS
    packed = jnp.pad(bias_row, ((0, 23), (0, 0))).astype(F32)
    packed += jnp.pad(mem_mu, ((1, 23 - heads), (0, edge))).astype(F32)
    packed += jnp.pad(mem_sig, ((1 + heads, 23 - 2 * heads), (0, edge))).astype(F32)
    line = jnp.arange(24)[:, None]
    for k, vector in enumerate((ln1_gain, ln1_bias, out_bias, ln2_gain, ln2_bias, ff_out_bias, ff_in_bias)):
        packed += jnp.where(line == 16 + k, vector.astype(F32)[None, :], 0.0)

    turned_weight = jnp.transpose(qkv_weight, (1, 2, 0)).reshape(3 * width, model)
    (
        qkv, first_cols, flat_a, flat_b, logsum, values, probes, key_states, key_end, state_rows,
        *mixed, in_bias, far_in, far_out, far_weight,
    ) = forward(seg_lengths, inputs, packed, turned_weight, out_weight, ff_in, ff_out, heads)
    flat = lambda array: array.reshape((shards - 1, slices) + array.shape[4:])
    outputs, grad_residual, *rest = middle(
        inputs, cotangent, mixed, out_weight, flat(far_weight), packed, in_bias,
        ff_in.reshape(slices, rows, hidden_part), ff_out.reshape(slices, rows, model), flat(far_in), flat(far_out),
    )
    grad_mixed, (ff_in_part, ff_out_part, out_weight_part, sums, in_bias_part) = rest[:4], rest[4:]
    paired = [part.reshape(units // 2, UNIT, width) for part in grad_mixed]
    plane = lambda array: array.reshape((shards, 2, 2, 2) + array.shape[2:])
    grads, probe_grad, *parts = backward(
        seg_lengths, qkv, paired, logsum, values, probes, key_states, key_end, state_rows, plane(ff_in_part),
        plane(ff_out_part), plane(out_weight_part), heads,
    )
    for bit in outer:
        parts = [added(part, exchange(part, "dp", bit)) for part in parts]
    input_grad, whole_in, whole_out, whole_weight, whole_qkv, shared, owned = tail(
        grads, first_cols, flat_a, flat_b, grad_residual, inputs, packed, parts, sums, in_bias_part, probe_grad,
        outer, heads,
    )
    ff_in_sum, ff_out_sum, out_weight_sum, qkv_weight_sum = finish(
        whole_in.reshape(model, hidden_part), whole_out.reshape(hidden_part, model),
        whole_weight.reshape((slices,) + whole_weight.shape[3:]), whole_qkv.reshape(model, 3 * width), width,
    )
    return (
        outputs, input_grad, shared[0], shared[1], jnp.transpose(qkv_weight_sum, (2, 0, 1)),
        owned[8].reshape(3, LANES)[:, :width], out_weight_sum, shared[2], owned[:heads, :BASIS],
        owned[heads : 2 * heads, :BASIS], shared[3], shared[4], ff_in_sum, owned[9, :hidden_part], ff_out_sum, shared[5],
    )


def solution(mesh):
    rows, whole = P(("dp", "head"), None), P()
    return jax.shard_map(
        local,
        mesh=mesh,
        in_specs=(
            rows, P("dp", None), whole, whole, P(None, None, "head"), P(None, "head"), P("head", None), whole,
            P("head", None), P("head", None), whole, whole, P(None, "head"), P("head"), P("head", None), whole, rows,
        ),
        out_specs=(
            rows, rows, whole, whole, P(None, None, "head"), P(None, "head"), P("head", None), whole,
            P("head", None), P("head", None), whole, whole, P(None, "head"), P("head"), P("head", None), whole,
        ),
        check_vma=False,
    )
```

profile of v0, /device:TPU:0, one launch (start us, length us, event | category | flops | bytes accessed | tf_op | source)
XLA Modules:
  0.0 304.2 jit_solution(3565649120006059109)
XLA Ops:
  0.7 0.7 pad_bitcast_fusion
  1.4 0.7 convert_element_type.41
  2.1 0.7 convert_element_type.42
  2.8 0.7 convert_element_type.43
  3.4 0.7 convert_element_type.44
  4.1 0.7 convert_element_type.45
  4.8 0.7 convert_element_type.47
  5.5 0.7 convert_element_type.46
  6.2 1.4 select_add_fusion.packed.vectors
  7.6 96.2 %forward.1 = (bf16[2,4,256,768]{3,2,1,0:T(8,128)(2,1)}, bf16[768,1024]{1,0:T(8,128)(2,1)}, bf16[768,768]{1,0:T(8,128)(2,1)}, bf16[768,768]{1,0:T(8,128)(2,1)}, f...) custom-call(s32[1,8]{1,0:T(1,128)} %seg_lengths.3, ...), custom_call_target="tpu_custom_call" | custom-call | tf_op jit(solution)/shard_map/forward/pallas_call | solution.py:447
  103.9 34.3 %middle.1 = (bf16[512,768]{1,0:T(8,128)(2,1)}, f32[512,768]{1,0:T(8,128)}, bf16[512,192]{1,0:T(8,128)(2,1)}, bf16[512,192]{1,0:T(8,128)(2,1)}, bf16[512,192]{1,0...) custom-call(bf16[512,768]{1,0:T(8,128)(2,1)} %source.5, ...), custom_call_target="tpu_custom_call" | custom-call | flops 16307453952 | bytes 31457280 | tf_op jit(solution)/shard_map/middle/pallas_call | solution.py:658
  138.1 93.5 %backward.1 = (bf16[2,4,256,768]{3,2,1,0:T(8,128)(2,1)}, f32[2,8,512]{2,1,0:T(8,128)}, bf16[96,768]{1,0:T(8,128)(2,1)}, bf16[96,768]{1,0:T(8,128)(2,1)}, bf16[32,768]{1,0:T(8,128)(2,1)}) custom-call(s32[1,8]{1,0:T(1,128)} %seg_lengths.3, bf16[2,4,256,768]{3,2,1,0:T(8,128)(2,1)} %get-tuple-element.70.qkv, bf16[2,256,192]{2,1,0:T(8,128)(2,1)} %bitcast.35, ...), custom_call_target="tpu_custom_call" | custom-call | tf_op jit(solution)/shard_map/backward/pallas_call | solution.py:976
  231.7 57.9 %tail.1 = (bf16[512,768]{1,0:T(8,128)(2,1)}, bf16[2,2,2,96,768]{4,3,2,1,0:T(8,128)(2,1)}, bf16[2,2,2,96,768]{4,3,2,1,0:T(8,128)(2,1)}, bf16[2,2,2,32,768]{4,3,2,...) custom-call(bf16[2,4,256,768]{3,2,1,0:T(8,128)(2,1)} %get-tuple-element.84.grads, ...), custom_call_target="tpu_custom_call" | custom-call | tf_op jit(solution)/shard_map/tail/pallas_call | solution.py:1182
  289.5 1.4 slice_reduce_fusion.1
  290.9 1.4 fusion
  292.3 0.6 reshape_squeeze.3
  292.9 1.7 slice_reduce_fusion
  294.7 1.3 copy-done
  296.0 1.3 copy-done.1
  297.2 1.2 copy-done.2
  298.4 1.0 copy-done.3
  299.4 3.7 %finish.1 = (f32[768,768]{1,0:T(8,128)}, f32[768,768]{1,0:T(8,128)}, f32[192,768]{1,0:T(8,128)}, f32[3,192,768]{2,1,0:T(8,128)}) custom-call(bf16[768,768]{1,0:T(8,128)(2,1)S(1)} %bitcast.25, bf16[768,768]{1,0:T(8,128)(2,1)S(1)} %bitcast.26, bf16[8,32,768]{2,1,0:T(8,128)(2,1)S(1)} %bitcast.28, bf16[768,576]{1,0:T(8,128)(2,1)S(1)} %bitcast.27), custom_call_target="tpu_custom_call" | custom-call | tf_op jit(solution)/shard_map/finish/pallas_call | solution.py:529
  303.1 0.0 copy-done.4
  303.1 0.9 copy.37
  (10 shorter events, 0.0 us)
Async XLA Ops:
  294.7 1.3 copy-start
  295.9 1.3 copy-start.1
  297.2 1.2 copy-start.2
  298.4 1.0 copy-start.3
  299.4 3.7 %copy-start.4 = (bf16[512,768]{1,0:T(8,128)(2,1)S(1)}, bf16[512,768]{1,0:T(8,128)(2,1)}, u32[]{:S(2)}) copy-start(bf16[512,768]{1,0:T(8,128)(2,1)} %get-tuple-element.139) | copy-start | bytes 2359300
where the time goes:
time: 308 us; the launch traced here: 304 us
  Pallas kernels  286 us (93%)
  local copies, waits for them, and re-layouts  11.5 us (4%)
  other arithmetic  6.25 us (2%)
    pallas_call x1, Pallas kernels, forward(): pl.pallas_call(functools.partial(forward_kernel, heads), in_specs=[pl.Blo...  96.2 us
    pallas_call x1, Pallas kernels, backward(): pl.pallas_call(functools.partial(backward_kernel, heads), in_specs=[pl.Bl...  93.5 us
    pallas_call x1, Pallas kernels, tail(): pl.pallas_call(functools.partial(tail_kernel, heads, outer), in_specs=[vm...  57.9 us
    pallas_call x1, Pallas kernels, middle(): pl.pallas_call(middle_kernel, grid_spec=pltpu.PrefetchScalarGridSpec(num_...  34.3 us
    unnamed x13, local copies, waits for them, and re-layouts  6.32 us

commit v1 on v0

--- a/solution.py
+++ b/solution.py
@@ -47,7 +47,7 @@
     joined = np.concatenate([solve @ contract, solve[:, LIVE:]], axis=1)
     high, low = split_table(joined)
     forward = np.concatenate([high, high, low], axis=1)
-    backward = np.concatenate([high.T, high.T, low.T], axis=1)
+    backward = np.ascontiguousarray(high.T)
     return forward, backward
 
 
@@ -95,11 +95,12 @@
 
 
 def advance_values(table, value):
-    joined = BASIS + LIVE if table.shape[0] == BASIS else BASIS
-    high, low = table[:BASIS, :BASIS], table[:BASIS, 2 * joined : 2 * joined + BASIS]
-    value_high = value.astype(BF16)
-    value_low = (value - value_high.astype(F32)).astype(BF16)
-    return dot(high, value_high) + dot(high, value_low) + dot(low, value_high)
+    return dot(table[:BASIS, :BASIS], value.astype(BF16))
+
+
+def logits_of(probes, query):
+    parts = dot(jnp.concatenate(split_rows(probes), axis=0), query, ((1,), (1,)))
+    return parts[0:8] + parts[8:16] + parts[16:24]
 
 
 def segments_of(lengths, run, units):
@@ -170,7 +171,7 @@
     qkv_out, first_cols_out, flat_a_out, flat_b_out, logsum, values, probes, key_states, key_end, rows,
     mixed_0, mixed_1, mixed_2, mixed_3, in_bias, far_in, far_out, far_weight,
     qkv, first_rows, first_cols, flats, near, far, far_flat, small, far_row, bias_row, weight_mine, memory, sums, value_states, carried, value_ends, value_ins,
-    projs, proj_ins, cols, discrete, mixed, mixed_in, send, recv, local_sems,
+    projs, proj_ins, cols, keys, discrete, mixed, mixed_in, send, recv, local_sems,
 ):
     own_rows, model = source.shape
     width = heads * HEAD_DIM
@@ -315,11 +316,18 @@
         psi_high = psi.astype(BF16)
         psi_low = (psi - psi_high.astype(F32)).astype(BF16)
         pairs = qkv[k, at(b), :, LANES : 3 * LANES]
-        fresh = dot(psi_high, pairs) + dot(psi_low, pairs)
+        exact = dot(psi_high, pairs[:, :LANES]) + dot(psi_low, pairs[:, :LANES])
+        fresh = jnp.concatenate([exact, dot(psi_high, pairs[:, LANES:])], axis=1)
         gathered = fresh if b == 0 else jnp.where(start == b, 0.0, sums[k]) + fresh
         sums[k] = gathered
         stacked = jnp.concatenate([now, gathered * term_scale(length)], axis=0)
-        later = dot(table[...], split3(stacked))
+        later = jnp.concatenate(
+            [
+                dot(table[...], split3(stacked[:, :LANES])),
+                dot(table[:, : BASIS + LIVE], stacked[:, LANES:].astype(BF16)),
+            ],
+            axis=1,
+        )
         memory[k] = jnp.where(start + length == b + 1, later, now)
         return carry
 
@@ -333,16 +341,19 @@
         return carry
 
     def attend(b, k, carry):
-        cols[k, b] = qkv[k, at(b), :, 2 * LANES : 3 * LANES].astype(F32).T.astype(BF16)
+        cols[k, :, b * UNIT : (b + 1) * UNIT] = qkv[k, at(b), :, 2 * LANES : 3 * LANES].astype(F32).T.astype(BF16)
+        keys[k, b * UNIT : (b + 1) * UNIT] = qkv[k, at(b), :, LANES : 2 * LANES]
         query = qkv[k, at(b), :, 0:LANES].astype(F32) * root
         lane_head = lax.broadcasted_iota(jnp.int32, (UNIT, LANES), 1) // HEAD_DIM
         causal = lax.broadcasted_iota(jnp.int32, (UNIT, UNIT), 0) <= lax.broadcasted_iota(
             jnp.int32, (UNIT, UNIT), 1
         )
         away = [jnp.where(starts[b] <= j, 0.0, 1e30) for j in range(b)] + [0.0]
+        owns = jnp.concatenate([jnp.where(lane_head == h, query, 0.0).astype(BF16) for h in range(heads)], axis=0)
+        seen = (b + 1) * UNIT
+        products = dot(keys[k, :seen], owns, ((1,), (1,)))
         for h in range(heads):
-            own = jnp.where(lane_head == h, query, 0.0).astype(BF16)
-            scores = [dot(qkv[k, at(j), :, LANES : 2 * LANES], own, ((1,), (1,))) for j in range(b + 1)]
+            scores = [products[j * UNIT : (j + 1) * UNIT, h * UNIT : (h + 1) * UNIT] for j in range(b + 1)]
             scores[b] = jnp.where(causal, scores[b], -1e30)
             highest = functools.reduce(
                 jnp.maximum, [jnp.max(s, axis=0, keepdims=True) - away[j] for j, s in enumerate(scores)]
@@ -350,7 +361,7 @@
             weights = [jnp.exp(s - (highest + away[j])) for j, s in enumerate(scores)]
             total = sum(jnp.sum(w, axis=0, keepdims=True) for w in weights)
             span = slice(h * HEAD_DIM, (h + 1) * HEAD_DIM)
-            part = sum(dot(cols[k, j, span], weights[j].astype(BF16)) for j in range(b + 1))
+            part = dot(cols[k, span, :seen], jnp.concatenate([w.astype(BF16) for w in weights], axis=0))
             discrete[k, b, span] = part * (1.0 / total)
             logsum[k, b, h : h + 1] = highest + jnp.log(total)
         return carry
@@ -372,7 +383,7 @@
     def read(rel, k, carry):
         b = at(rel)
         query = qkv[k, rel, :, 0:LANES]
-        logits = sum(dot(part, query, ((1,), (1,))) for part in split_rows(probes[k, b]))
+        logits = logits_of(probes[k, b], query)
         location, variance = read_parts(logits, heads)
         fall = -0.5 / variance
         peak = WIDTH * lax.rsqrt(variance)
@@ -412,12 +423,12 @@
         for copy in state_copies[1 - k]:
             copy.wait_recv()
         seen_value(k, 0)
-        for rel in (2, 3, 0, 1):
-            read(rel, k, 0)
-            if rel == 3:
-                mixed_copies[k] = go(mixed.at[k, half:], mixed_in.at[k], "head", 1)
-        if k == 1:
-            advance(2, 3)
+        read(2, k, 0)
+        read(3, k, 0)
+        mixed_copies[k] = go(mixed.at[k, half:], mixed_in.at[k], "head", 1)
+    advance(2, 3)
+    lax.fori_loop(0, 2, functools.partial(read, 0), 0)
+    lax.fori_loop(0, 2, functools.partial(read, 1), 0)
     advance(3, 3)
     mixed_0[...] = mixed[0, :half].reshape(own_rows, width)
     mixed_2[...] = mixed[1, :half].reshape(own_rows, width)
@@ -485,7 +496,8 @@
             pltpu.VMEM((2, BASIS, width), BF16),
             pltpu.VMEM((2, 32, LANES), F32),
             pltpu.VMEM((2, 32, LANES), F32),
-            pltpu.VMEM((2, units, LANES, UNIT), BF16),
+            pltpu.VMEM((2, LANES, units * UNIT), BF16),
+            pltpu.VMEM((2, units * UNIT, LANES), BF16),
             pltpu.VMEM((2, units, width, UNIT), F32),
             pltpu.VMEM((2, units, UNIT, width), BF16),
             pltpu.VMEM((2, units // 2, UNIT, width), BF16),
@@ -545,7 +557,7 @@
             jax.ShapeDtypeStruct((model, columns), F32), jax.ShapeDtypeStruct((hidden_part, model), F32),
             jax.ShapeDtypeStruct((width, model), F32), jax.ShapeDtypeStruct((3, width, model), F32),
         ],
-        compiler_params=pltpu.CompilerParams(vmem_limit_bytes=48 << 20),
+        compiler_params=pltpu.CompilerParams(vmem_limit_bytes=62 << 20),
         name="finish",
     )(given_in, given_out, given_weight, given_qkv)
 
@@ -594,8 +606,8 @@
             in_now[j * rows : (j + 1) * rows] = far_in[0, j]
             out_now[j * rows : (j + 1) * rows] = far_out[0, j]
 
-    half = hidden_part // 2
-    for t in range(2):
+    half = hidden_part
+    for t in range(1):
         span = slice(t * half, (t + 1) * half)
         hidden = dot(second[...], in_now[:, span]) + in_bias[r, 0:1, span]
         cube = hidden * hidden
@@ -704,7 +716,7 @@
 def backward_kernel(
     heads, seg_lengths, qkv, gm_0, gm_1, gm_2, gm_3, logsum, values, probes, key_states, key_end, rows, table,
     grad_in, grad_out, grad_weight, out, probe_grad, slice_in, slice_out, slice_weight,
-    given, query_grad, memory_grad, row_grad, value_carried, value_back, value_in, row_back, row_in, carried, spread, key_grad, value_grad, cols,
+    given, query_grad, memory_grad, row_grad, value_carried, value_back, value_in, row_back, row_in, carried, spread, key_grad, value_grad, cols, keys, vals,
     keep_in, keep_out, keep_weight, core_in, core_out, core_weight, one_in, one_out, one_weight,
     two_in, two_out, two_weight, z_in, z_out, z_weight, send, recv, local_sems,
 ):
@@ -778,7 +790,7 @@
         query = qkv[k, rel, :, 0:LANES]
         full = given_of(k, b)
         probe = probes[k, b]
-        logits = sum(dot(part, query, ((1,), (1,))) for part in split_rows(probe))
+        logits = logits_of(probe, query)
         location, variance = read_parts(logits, heads)
         inverse = 1.0 / variance
         fall = -0.5 * inverse
@@ -808,8 +820,8 @@
         )
         padded = jnp.concatenate([grad_logits, jnp.zeros((120, UNIT), F32)], axis=0)
         probe_cols = jnp.concatenate([probe, jnp.zeros((120, LANES), F32)], axis=0).T
-        query_grad[k, b] = dot(probe_cols, padded, precision=HIGHEST)[:width]
-        fresh = jnp.where(mask, dot(grad_logits, query.astype(F32), precision=HIGHEST), 0.0) * root
+        query_grad[k, b] = dot(probe_cols.astype(BF16), padded.astype(BF16))[:width]
+        fresh = jnp.where(mask, dot(grad_logits.astype(BF16), query), 0.0) * root
         memory_grad[k, b] = total
         row_grad[k, b] = fresh
         return carry
@@ -820,7 +832,8 @@
             row_back[k, 8 * i : 8 * i + 8] = jnp.zeros((8, LANES), F32)
         for b in range(units - 1, -1, -1):
             fresh, total = row_grad[k, b], memory_grad[k, b]
-            probe += dot(fresh, key_states[k, b].astype(F32), ((1,), (1,)), HIGHEST)
+            if b > 0:
+                probe += dot(fresh.astype(BF16), key_states[k, b], ((1,), (1,)))
             for i in range(4):
                 row_back[k, 8 * i : 8 * i + 8] += jnp.where(orders[b] == i, fresh, 0.0)
             if b < units - 1:
@@ -845,51 +858,58 @@
         away = [jnp.where(starts[b] <= j, 0.0, 1e30) for j in range(b)] + [0.0]
         owns = [jnp.where(lane_head == h, query, 0.0).astype(BF16) for h in range(heads)]
         own_givens = [jnp.where(lane_head == h, full, 0.0).astype(BF16) for h in range(heads)]
+        own_all = jnp.concatenate(owns, axis=0)
+        given_all = jnp.concatenate(own_givens, axis=0)
+        seen = (b + 1) * UNIT
+        scores = dot(keys[k, :seen], own_all, ((1,), (1,)))
+        grad_probs = dot(vals[k, :seen], given_all, ((1,), (1,)))
         grads, probs = [], []
         for h in range(heads):
             prob_h, product_h = [], []
             inner = jnp.zeros((1, UNIT), F32)
             for j in range(b + 1):
-                score = dot(qkv[k, at(j), :, LANES : 2 * LANES], owns[h], ((1,), (1,)))
+                tile = (slice(j * UNIT, (j + 1) * UNIT), slice(h * UNIT, (h + 1) * UNIT))
+                score = scores[tile]
                 if j == b:
                     score = jnp.where(causal, score, -1e30)
                 prob = jnp.exp(score - (logsum[k, b, h : h + 1] + away[j]))
-                product = prob * dot(qkv[k, at(j), :, 2 * LANES : 3 * LANES], own_givens[h], ((1,), (1,)))
+                product = prob * grad_probs[tile]
                 inner += jnp.sum(product, axis=0, keepdims=True)
                 prob_h.append(prob)
                 product_h.append(product)
             span = slice(h * HEAD_DIM, (h + 1) * HEAD_DIM)
             grad_h = [(product_h[j] - prob_h[j] * inner).astype(BF16) for j in range(b + 1)]
-            result = sum(dot(cols[k, j, span], grad_h[j]) for j in range(b + 1))
+            result = dot(cols[k, span, :seen], jnp.concatenate(grad_h, axis=0))
             query_grad[k, b, span] = query_grad[k, b, span] + result * root
             grads.append(grad_h)
             probs.append([prob.astype(BF16) for prob in prob_h])
-        own_all = jnp.concatenate(owns, axis=0)
-        given_all = jnp.concatenate(own_givens, axis=0)
+        fresh_keys = dot(jnp.concatenate([jnp.concatenate(g, axis=0) for g in grads], axis=1), own_all)
+        fresh_vals = dot(jnp.concatenate([jnp.concatenate(p, axis=0) for p in probs], axis=1), given_all)
         for j in range(b + 1):
-            keys = dot(jnp.concatenate([grads[h][j] for h in range(heads)], axis=1), own_all)
-            vals = dot(jnp.concatenate([probs[h][j] for h in range(heads)], axis=1), given_all)
+            part = slice(j * UNIT, (j + 1) * UNIT)
             if b == units - 1:
-                key_grad[k, j], value_grad[k, j] = keys, vals
+                key_grad[k, j], value_grad[k, j] = fresh_keys[part], fresh_vals[part]
             else:
-                key_grad[k, j] += keys
-                value_grad[k, j] += vals
+                key_grad[k, j] += fresh_keys[part]
+                value_grad[k, j] += fresh_vals[part]
         return carry
 
     def carry_back(k, total, units_before):
-        moved = dot(table[...], split3(total))
+        moved = dot(table[...], total.astype(BF16))
         return moved[:BASIS], (moved[BASIS:] * term_scale(units_before)).astype(BF16)
 
     def end_back(k, carry):
         row = jnp.where(run == 0, row_in[k], 0.0)
         value = jnp.where(run == 0, value_in[k].astype(F32), 0.0)
-        grad_keys = dot(rows[k], row, ((0,), (0,)), HIGHEST)
+        grad_keys = dot(rows[k].astype(BF16), row.astype(BF16), ((0,), (0,)))
         total = jnp.concatenate([grad_keys, value, jnp.zeros((BASIS, LANES - width), F32)], axis=1)
         carried[k], spread[k] = carry_back(k, total, lengths[units - 1])
         seen = dot(row, key_end[k], ((1,), (1,)), HIGHEST)
         gained = seen[24:32]
         for i in (2, 1, 0):
-            gained = three_pass(gained, table[:BASIS, :BASIS], table[:BASIS, 2 * BASIS : 3 * BASIS])
+            high = gained.astype(BF16)
+            low = (gained - high.astype(F32)).astype(BF16)
+            gained = dot(high, table[:BASIS]) + dot(low, table[:BASIS])
             gained = gained + seen[8 * i : 8 * i + 8]
         probe_grad[k] += gained
         return carry
@@ -906,7 +926,7 @@
         out[k, at(b), :, LANES : 2 * LANES] = (key_grad[k, b] + pair_grad[:, :LANES]).astype(BF16)
         out[k, at(b), :, 2 * LANES :] = (value_grad[k, b] + pair_grad[:, LANES:]).astype(BF16)
         if b > 0:
-            grad_keys = dot(rows[k, 0:8], row_grad[k, b], ((0,), (0,)), HIGHEST)
+            grad_keys = dot(rows[k, 0:8].astype(BF16), row_grad[k, b].astype(BF16), ((0,), (0,)))
             total = carried[k] + jnp.concatenate([grad_keys, memory_grad[k, b]], axis=1)
             moved, spread_now = carry_back(k, total, lengths[b - 1])
             carried[k] = jnp.where(start == b, moved, carried[k])
@@ -918,7 +938,10 @@
 
     def turn(k, carry):
         for b in range(units):
-            cols[k, b] = qkv[k, at(b), :, LANES : 2 * LANES].astype(F32).T.astype(BF16)
+            part = slice(b * UNIT, (b + 1) * UNIT)
+            keys[k, part] = qkv[k, at(b), :, LANES : 2 * LANES]
+            vals[k, part] = qkv[k, at(b), :, 2 * LANES : 3 * LANES]
+            cols[k, :, part] = qkv[k, at(b), :, LANES : 2 * LANES].astype(F32).T.astype(BF16)
         return carry
 
     lax.fori_loop(0, 2, turn, 0)
@@ -992,7 +1015,9 @@
             pltpu.VMEM((2, LIVE, 2 * LANES), BF16),
             pltpu.VMEM((2, units, UNIT, LANES), F32),
             pltpu.VMEM((2, units, UNIT, LANES), F32),
-            pltpu.VMEM((2, units, LANES, UNIT), BF16),
+            pltpu.VMEM((2, LANES, units * UNIT), BF16),
+            pltpu.VMEM((2, units * UNIT, LANES), BF16),
+            pltpu.VMEM((2, units * UNIT, LANES), BF16),
         ]
         + [pltpu.VMEM((4, 2, 2) + part, BF16) for part in slices]
         + [pltpu.VMEM((4, 2, 2) + part, BF16) for part in slices]
@@ -1253,9 +1278,8 @@
     packed = jnp.pad(bias_row, ((0, 23), (0, 0))).astype(F32)
     packed += jnp.pad(mem_mu, ((1, 23 - heads), (0, edge))).astype(F32)
     packed += jnp.pad(mem_sig, ((1 + heads, 23 - 2 * heads), (0, edge))).astype(F32)
-    line = jnp.arange(24)[:, None]
-    for k, vector in enumerate((ln1_gain, ln1_bias, out_bias, ln2_gain, ln2_bias, ff_out_bias, ff_in_bias)):
-        packed += jnp.where(line == 16 + k, vector.astype(F32)[None, :], 0.0)
+    vectors = jnp.concatenate([ln1_gain, ln1_bias, out_bias, ln2_gain, ln2_bias, ff_out_bias, ff_in_bias])
+    packed += jnp.pad(vectors.reshape(7, model), ((16, 1), (0, 0))).astype(F32)
 
     turned_weight = jnp.transpose(qkv_weight, (1, 2, 0)).reshape(3 * width, model)
     (

time: 308 us -> 284 us (0.922)
  Pallas kernels: 286 us -> 266 us
  other arithmetic: 6.25 us -> 1.36 us
    pallas_call x1, Pallas kernels: 93.5 us -> 83.1 us  [backward(): pl.pallas_call(functools.partial(backward_kernel, heads), in_specs=[pl.Bl...]
    pallas_call x1, Pallas kernels: 34.3 us -> 29.1 us  [middle(): pl.pallas_call(middle_kernel, grid_spec=pltpu.PrefetchScalarGridSpec(num_...]
    convert_element_type x7 -> x0, other arithmetic: 4.78 us -> none  [local(): packed += jnp.where(line == 16 + k, vector.astype(F32)[None, :], 0.0)]
    pallas_call x1, Pallas kernels: 57.9 us -> 54.3 us  [tail(): pl.pallas_call(functools.partial(tail_kernel, heads, outer), in_specs=[vm...]
    unnamed x13 -> x11, local copies, waits for them, and re-layouts: 6.32 us -> 6.7 us
where the time goes in v1:
time: 284 us; the launch traced here: 279 us
  Pallas kernels  266 us (94%)
  local copies, waits for them, and re-layouts  11.4 us (4%)
    pallas_call x1, Pallas kernels, forward(): pl.pallas_call(functools.partial(forward_kernel, heads), in_specs=[pl.Blo...  93.3 us
    pallas_call x1, Pallas kernels, backward(): pl.pallas_call(functools.partial(backward_kernel, heads), in_specs=[pl.Bl...  83.1 us
    pallas_call x1, Pallas kernels, tail(): pl.pallas_call(functools.partial(tail_kernel, heads, outer), in_specs=[vm...  54.3 us
    pallas_call x1, Pallas kernels, middle(): pl.pallas_call(middle_kernel, grid_spec=pltpu.PrefetchScalarGridSpec(num_...  29.1 us
    unnamed x11, local copies, waits for them, and re-layouts  6.7 us
    pallas_call x1, Pallas kernels, finish(): pl.pallas_call(finish_kernel, grid=(3,), in_specs=[pl.BlockSpec((model //...  5.79 us

profile of v1, /device:TPU:0, one launch (start us, length us, event | category | flops | bytes accessed | tf_op | source)
XLA Modules:
  0.0 279.2 jit_solution(11396274507588451344)
XLA Ops:
  0.6 0.7 pad_bitcast_fusion
  1.4 0.9 dynamic-update-slice
  2.2 0.8 dynamic-update-slice.1
  3.1 0.9 dynamic-update-slice.2
  3.9 0.9 dynamic-update-slice.3
  4.8 0.9 dynamic-update-slice.4
  5.6 0.8 dynamic-update-slice.5
  6.5 0.9 dynamic-update-slice.6
  7.4 1.4 convert_add_fusion.packed.vectors
  8.7 93.3 %forward.1 = (bf16[2,4,256,768]{3,2,1,0:T(8,128)(2,1)}, bf16[768,1024]{1,0:T(8,128)(2,1)}, bf16[768,768]{1,0:T(8,128)(2,1)}, bf16[768,768]{1,0:T(8,128)(2,1)}, f...) custom-call(s32[1,8]{1,0:T(1,128)} %seg_lengths.3, ...), custom_call_target="tpu_custom_call" | custom-call | tf_op jit(solution)/shard_map/forward/pallas_call | solution.py:458
  102.0 29.1 %middle.1 = (bf16[512,768]{1,0:T(8,128)(2,1)}, f32[512,768]{1,0:T(8,128)}, bf16[512,192]{1,0:T(8,128)(2,1)}, bf16[512,192]{1,0:T(8,128)(2,1)}, bf16[512,192]{1,0...) custom-call(bf16[512,768]{1,0:T(8,128)(2,1)} %source.5, ...), custom_call_target="tpu_custom_call" | custom-call | flops 16307453952 | bytes 31457280 | tf_op jit(solution)/shard_map/middle/pallas_call | solution.py:670
  131.2 83.1 %backward.1 = (bf16[2,4,256,768]{3,2,1,0:T(8,128)(2,1)}, f32[2,8,512]{2,1,0:T(8,128)}, bf16[96,768]{1,0:T(8,128)(2,1)}, bf16[96,768]{1,0:T(8,128)(2,1)}, bf16[32,768]{1,0:T(8,128)(2,1)}) custom-call(s32[1,8]{1,0:T(1,128)} %seg_lengths.3, bf16[2,4,256,768]{3,2,1,0:T(8,128)(2,1)} %get-tuple-element.70.qkv, bf16[2,256,192]{2,1,0:T(8,128)(2,1)} %bitcast.35, ...), custom_call_target="tpu_custom_call" | custom-call | tf_op jit(solution)/shard_map/backward/pallas_call | solution.py:999
  214.3 54.3 %tail.1 = (bf16[512,768]{1,0:T(8,128)(2,1)}, bf16[2,2,2,96,768]{4,3,2,1,0:T(8,128)(2,1)}, bf16[2,2,2,96,768]{4,3,2,1,0:T(8,128)(2,1)}, bf16[2,2,2,32,768]{4,3,2,...) custom-call(bf16[2,4,256,768]{3,2,1,0:T(8,128)(2,1)} %get-tuple-element.84.grads, ...), custom_call_target="tpu_custom_call" | custom-call | tf_op jit(solution)/shard_map/tail/pallas_call | solution.py:1207
  268.5 0.0 copy-start
  268.5 1.4 fusion
  270.0 1.8 slice_reduce_fusion
  271.7 0.6 reshape_squeeze.3
  272.3 5.8 %finish.1 = (f32[768,768]{1,0:T(8,128)}, f32[768,768]{1,0:T(8,128)}, f32[192,768]{1,0:T(8,128)}, f32[3,192,768]{2,1,0:T(8,128)}) custom-call(bf16[768,768]{1,0:T(8,128)(2,1)} %bitcast.28, bf16[768,768]{1,0:T(8,128)(2,1)} %bitcast.29, bf16[8,32,768]{2,1,0:T(8,128)(2,1)} %bitcast.34, bf16[768,576]{1,0:T(8,128)(2,1)} %bitcast.32), custom_call_target="tpu_custom_call" | custom-call | tf_op jit(solution)/shard_map/finish/pallas_call | solution.py:541
  278.1 0.0 copy-done
  278.1 0.9 copy.44
  (3 shorter events, 0.0 us)
Async XLA Ops:
  268.5 9.6 %copy-start = (bf16[512,768]{1,0:T(8,128)(2,1)S(1)}, bf16[512,768]{1,0:T(8,128)(2,1)}, u32[]{:S(2)}) copy-start(bf16[512,768]{1,0:T(8,128)(2,1)} %get-tuple-element.135) | copy-start | bytes 2359300

commit v2 on v1

--- a/solution.py
+++ b/solution.py
@@ -220,12 +220,31 @@
     out_mine = ff_out.at[pl.ds(pl.multiple_of(place * slice_rows, 16), slice_rows)]
     gathers = ((far_in, 2, 4), (far_weight, 2, 4), (far_out, 4, 2))
     stage = {}
-    for r in (1, 2, 3):
+
+    def send_chunk(r):
         stage[r] = [
             go(in_mine, far_in.at[r - 1, y, x, c], "head", r),
             go(weight_mine, far_weight.at[r - 1, y, x, c], "head", r),
             go(out_mine, far_out.at[r - 1, y, x, c], "head", r),
         ]
+
+    def advance(r, step):
+        for copy in stage[r]:
+            copy.wait_recv()
+        stage[r] = []
+        for array, first, second in gathers:
+            block = array.at[r - 1]
+            if step == 1:
+                part, bit = block.at[y, x, c], first
+            elif step == 2:
+                part, bit = (block.at[y, :, c] if first == 2 else block.at[:, x, c]), second
+            else:
+                part, bit = block.at[:, :, c], 1
+            stage[r].append(go(part, part, "dp", bit))
+
+    send_chunk(1)
+    send_chunk(2)
+    send_chunk(3)
     in_bias[0] = bias_row[...]
     bias_copies = [go(bias_row, in_bias.at[r], "head", r) for r in (1, 2, 3)]
 
@@ -256,20 +275,7 @@
         first_rows[own_rows + k * UNIT : own_rows + (k + 1) * UNIT] = near[part]
         project(0, half + k, small[0:1])
 
-    def advance(r, step):
-        for copy in stage[r]:
-            copy.wait_recv()
-        stage[r] = []
-        for array, first, second in gathers:
-            block = array.at[r - 1]
-            if step == 1:
-                part, bit = block.at[y, x, c], first
-            elif step == 2:
-                part, bit = (block.at[y, :, c] if first == 2 else block.at[:, x, c]), second
-            else:
-                part, bit = block.at[:, :, c], 1
-            stage[r].append(go(part, part, "dp", bit))
-
+    advance(1, 1)
     first_cols[:, own_rows:] = near[...].astype(F32).T.astype(BF16)
     core_copy.wait_recv()
     for i in range(8):
@@ -334,7 +340,7 @@
     def end_state(k, carry):
         key = memory[k, :, :LANES]
         key_end[k] = key
-        value_ends[k] = memory[k, :, LANES : LANES + width].astype(BF16)
+        value_ends[k] = memory[k, :, LANES : LANES + width].T.astype(BF16)
         seen = dot(rows[k], key, precision=HIGHEST)
         for i in range(4):
             projs[k, 8 * i : 8 * i + 8] = jnp.where(mask, seen[8 * i : 8 * i + 8], 0.0)
@@ -367,7 +373,7 @@
         return carry
 
     def seen_value(k, carry):
-        incoming = jnp.where(run > 0, value_ins[k].astype(F32), 0.0)
+        incoming = jnp.where(run > 0, value_ins[k].astype(F32), 0.0).T
         carried[:, :width] = incoming
         carried[:, width:] = jnp.zeros((BASIS, LANES - width), F32)
         for b in range(units):
@@ -398,7 +404,7 @@
         mixed[k, rel] = jnp.concatenate(parts, axis=0).T.astype(BF16)
         return carry
 
-    advance(1, 1)
+    advance(1, 2)
     state_copies = []
     for k in range(2):
         for b in range(units):
@@ -409,15 +415,17 @@
         ])
         if k == 0:
             advance(2, 1)
-            advance(1, 2)
-    advance(3, 1)
+            advance(3, 1)
+        if k == 1:
+            advance(1, 3)
     for b in range(units):
         lax.fori_loop(0, 2, functools.partial(attend, b), 0)
         if b == 0:
             advance(2, 2)
         if b == 2:
-            advance(1, 3)
             advance(3, 2)
+        if b == 3:
+            advance(2, 3)
     mixed_copies = [None, None]
     for k in (1, 0):
         for copy in state_copies[1 - k]:
@@ -426,10 +434,10 @@
         read(2, k, 0)
         read(3, k, 0)
         mixed_copies[k] = go(mixed.at[k, half:], mixed_in.at[k], "head", 1)
-    advance(2, 3)
+        if k == 1:
+            advance(3, 3)
     lax.fori_loop(0, 2, functools.partial(read, 0), 0)
     lax.fori_loop(0, 2, functools.partial(read, 1), 0)
-    advance(3, 3)
     mixed_0[...] = mixed[0, :half].reshape(own_rows, width)
     mixed_2[...] = mixed[1, :half].reshape(own_rows, width)
     for copy in mixed_copies:
@@ -492,8 +500,8 @@
             pltpu.VMEM((2, LIVE, 2 * LANES), F32),
             pltpu.VMEM((2, units, BASIS, LANES), F32),
             pltpu.VMEM((BASIS, LANES), F32),
-            pltpu.VMEM((2, BASIS, width), BF16),
-            pltpu.VMEM((2, BASIS, width), BF16),
+            pltpu.VMEM((2, width, BASIS), BF16),
+            pltpu.VMEM((2, width, BASIS), BF16),
             pltpu.VMEM((2, 32, LANES), F32),
             pltpu.VMEM((2, 32, LANES), F32),
             pltpu.VMEM((2, LANES, units * UNIT), BF16),
@@ -845,7 +853,7 @@
             if b > 0:
                 value_carried[k] = jnp.where(starts[b] == b, advance_values(table, before + total), before)
             else:
-                value_back[k] = (before + total)[:, :width].astype(BF16)
+                value_back[k] = (before + total)[:, :width].T.astype(BF16)
         probe_grad[k] = probe
         return carry
 
@@ -900,7 +908,7 @@
 
     def end_back(k, carry):
         row = jnp.where(run == 0, row_in[k], 0.0)
-        value = jnp.where(run == 0, value_in[k].astype(F32), 0.0)
+        value = jnp.where(run == 0, value_in[k].astype(F32), 0.0).T
         grad_keys = dot(rows[k].astype(BF16), row.astype(BF16), ((0,), (0,)))
         total = jnp.concatenate([grad_keys, value, jnp.zeros((BASIS, LANES - width), F32)], axis=1)
         carried[k], spread[k] = carry_back(k, total, lengths[units - 1])
@@ -1007,8 +1015,8 @@
             pltpu.VMEM((2, units, BASIS, LANES), F32),
             pltpu.VMEM((2, units, 8, LANES), F32),
             pltpu.VMEM((2, BASIS, LANES), F32),
-            pltpu.VMEM((2, BASIS, width), BF16),
-            pltpu.VMEM((2, BASIS, width), BF16),
+            pltpu.VMEM((2, width, BASIS), BF16),
+            pltpu.VMEM((2, width, BASIS), BF16),
             pltpu.VMEM((2, 32, LANES), F32),
             pltpu.VMEM((2, 32, LANES), F32),
             pltpu.VMEM((2, BASIS, 2 * LANES), F32),
@@ -1278,8 +1286,9 @@
     packed = jnp.pad(bias_row, ((0, 23), (0, 0))).astype(F32)
     packed += jnp.pad(mem_mu, ((1, 23 - heads), (0, edge))).astype(F32)
     packed += jnp.pad(mem_sig, ((1 + heads, 23 - 2 * heads), (0, edge))).astype(F32)
-    vectors = jnp.concatenate([ln1_gain, ln1_bias, out_bias, ln2_gain, ln2_bias, ff_out_bias, ff_in_bias])
-    packed += jnp.pad(vectors.reshape(7, model), ((16, 1), (0, 0))).astype(F32)
+    given = (ln1_gain, ln1_bias, out_bias, ln2_gain, ln2_bias, ff_out_bias, ff_in_bias)
+    line = sum(jnp.pad(vector.astype(F32), (k * model, (6 - k) * model)) for k, vector in enumerate(given))
+    packed += jnp.pad(line.reshape(7, model), ((16, 1), (0, 0)))
 
     turned_weight = jnp.transpose(qkv_weight, (1, 2, 0)).reshape(3 * width, model)
     (

time: 284 us -> 271 us (0.954)
  Pallas kernels: 266 us -> 259 us
  local copies, waits for them, and re-layouts: 11.4 us -> 5.38 us
    pallas_call x1, Pallas kernels: 83.1 us -> 75.8 us  [backward(): pl.pallas_call(functools.partial(backward_kernel, heads), in_specs=[pl.Bl...]
    unnamed x11 -> x5, local copies, waits for them, and re-layouts: 6.7 us -> 1.58 us
    pallas_call x1, Pallas kernels: 54.3 us -> 50.1 us  [tail(): pl.pallas_call(functools.partial(tail_kernel, heads, outer), in_specs=[vm...]
    pallas_call x1, Pallas kernels: 93.3 us -> 97.4 us  [forward(): pl.pallas_call(functools.partial(forward_kernel, heads), in_specs=[pl.Blo...]
where the time goes in v2:
time: 271 us; the launch traced here: 267 us
  Pallas kernels  259 us (96%)
  local copies, waits for them, and re-layouts  5.38 us (2%)
    pallas_call x1, Pallas kernels, forward(): pl.pallas_call(functools.partial(forward_kernel, heads), in_specs=[pl.Blo...  97.4 us
    pallas_call x1, Pallas kernels, backward(): pl.pallas_call(functools.partial(backward_kernel, heads), in_specs=[pl.Bl...  75.8 us
    pallas_call x1, Pallas kernels, tail(): pl.pallas_call(functools.partial(tail_kernel, heads, outer), in_specs=[vm...  50.1 us
    pallas_call x1, Pallas kernels, middle(): pl.pallas_call(middle_kernel, grid_spec=pltpu.PrefetchScalarGridSpec(num_...  29.5 us
    pallas_call x1, Pallas kernels, finish(): pl.pallas_call(finish_kernel, grid=(3,), in_specs=[pl.BlockSpec((model //...  5.79 us

profile of v2, /device:TPU:0, one launch (start us, length us, event | category | flops | bytes accessed | tf_op | source)
XLA Modules:
  0.0 267.1 jit_solution(70507994523871089)
XLA Ops:
  0.6 0.7 pad_bitcast_fusion
  1.3 0.8 convert_add_fusion
  2.2 1.4 pad_add_fusion.packed.vectors
  3.5 97.4 %forward.1 = (bf16[2,4,256,768]{3,2,1,0:T(8,128)(2,1)}, bf16[768,1024]{1,0:T(8,128)(2,1)}, bf16[768,768]{1,0:T(8,128)(2,1)}, bf16[768,768]{1,0:T(8,128)(2,1)}, f...) custom-call(s32[1,8]{1,0:T(1,128)} %seg_lengths.3, ...), custom_call_target="tpu_custom_call" | custom-call | tf_op jit(solution)/shard_map/forward/pallas_call | solution.py:466
  100.9 29.5 %middle.1 = (bf16[512,768]{1,0:T(8,128)(2,1)}, f32[512,768]{1,0:T(8,128)}, bf16[512,192]{1,0:T(8,128)(2,1)}, bf16[512,192]{1,0:T(8,128)(2,1)}, bf16[512,192]{1,0...) custom-call(bf16[512,768]{1,0:T(8,128)(2,1)} %source.5, ...), custom_call_target="tpu_custom_call" | custom-call | flops 16307453952 | bytes 31457280 | tf_op jit(solution)/shard_map/middle/pallas_call | solution.py:678
  130.4 75.8 %backward.1 = (bf16[2,4,256,768]{3,2,1,0:T(8,128)(2,1)}, f32[2,8,512]{2,1,0:T(8,128)}, bf16[96,768]{1,0:T(8,128)(2,1)}, bf16[96,768]{1,0:T(8,128)(2,1)}, bf16[32,768]{1,0:T(8,128)(2,1)}) custom-call(s32[1,8]{1,0:T(1,128)} %seg_lengths.3, bf16[2,4,256,768]{3,2,1,0:T(8,128)(2,1)} %get-tuple-element.70.qkv, bf16[2,256,192]{2,1,0:T(8,128)(2,1)} %bitcast.35, ...), custom_call_target="tpu_custom_call" | custom-call | tf_op jit(solution)/shard_map/backward/pallas_call | solution.py:1007
  206.3 50.1 %tail.1 = (bf16[512,768]{1,0:T(8,128)(2,1)}, bf16[2,2,2,96,768]{4,3,2,1,0:T(8,128)(2,1)}, bf16[2,2,2,96,768]{4,3,2,1,0:T(8,128)(2,1)}, bf16[2,2,2,32,768]{4,3,2,...) custom-call(bf16[2,4,256,768]{3,2,1,0:T(8,128)(2,1)} %get-tuple-element.84.grads, ...), custom_call_target="tpu_custom_call" | custom-call | tf_op jit(solution)/shard_map/tail/pallas_call | solution.py:1215
  256.4 0.0 copy-start
  256.4 1.4 fusion
  257.8 1.8 slice_reduce_fusion
  259.6 0.6 reshape_squeeze.3
  260.2 5.8 %finish.1 = (f32[768,768]{1,0:T(8,128)}, f32[768,768]{1,0:T(8,128)}, f32[192,768]{1,0:T(8,128)}, f32[3,192,768]{2,1,0:T(8,128)}) custom-call(bf16[768,768]{1,0:T(8,128)(2,1)} %bitcast.28, bf16[768,768]{1,0:T(8,128)(2,1)} %bitcast.29, bf16[8,32,768]{2,1,0:T(8,128)(2,1)} %bitcast.34, bf16[768,576]{1,0:T(8,128)(2,1)} %bitcast.32), custom_call_target="tpu_custom_call" | custom-call | tf_op jit(solution)/shard_map/finish/pallas_call | solution.py:549
  266.0 0.0 copy-done
  266.0 0.9 copy.37
  (2 shorter events, 0.0 us)
Async XLA Ops:
  256.4 9.6 %copy-start = (bf16[512,768]{1,0:T(8,128)(2,1)S(1)}, bf16[512,768]{1,0:T(8,128)(2,1)}, u32[]{:S(2)}) copy-start(bf16[512,768]{1,0:T(8,128)(2,1)} %get-tuple-element.135) | copy-start | bytes 2359300

commit v3 on v2

--- a/solution.py
+++ b/solution.py
@@ -168,10 +168,10 @@
 
 def forward_kernel(
     heads, seg_lengths, source, packed, weight, out_weight, table, ff_in, ff_out,
-    qkv_out, first_cols_out, flat_a_out, flat_b_out, logsum, values, probes, key_states, key_end, rows,
+    qkv_out, first_cols_out, flat_a_out, flat_b_out, values_out, key_states_out, key_end_out, logsum, probes, rows,
     mixed_0, mixed_1, mixed_2, mixed_3, in_bias, far_in, far_out, far_weight,
     qkv, first_rows, first_cols, flats, near, far, far_flat, small, far_row, bias_row, weight_mine, memory, sums, value_states, carried, value_ends, value_ins,
-    projs, proj_ins, cols, keys, discrete, mixed, mixed_in, send, recv, local_sems,
+    projs, proj_ins, cols, keys, discrete, mixed, mixed_in, values, key_states, key_end, send, recv, local_sems,
 ):
     own_rows, model = source.shape
     width = heads * HEAD_DIM
@@ -426,6 +426,7 @@
             advance(3, 2)
         if b == 3:
             advance(2, 3)
+    saved += set_out([(key_states, key_states_out), (key_end, key_end_out)], local_sems, 4)
     mixed_copies = [None, None]
     for k in (1, 0):
         for copy in state_copies[1 - k]:
@@ -436,6 +437,7 @@
         mixed_copies[k] = go(mixed.at[k, half:], mixed_in.at[k], "head", 1)
         if k == 1:
             advance(3, 3)
+    saved += set_out([(values, values_out)], local_sems, 6)
     lax.fori_loop(0, 2, functools.partial(read, 0), 0)
     lax.fori_loop(0, 2, functools.partial(read, 1), 0)
     mixed_0[...] = mixed[0, :half].reshape(own_rows, width)
@@ -466,17 +468,17 @@
     return pl.pallas_call(
         functools.partial(forward_kernel, heads),
         in_specs=[pl.BlockSpec(memory_space=pltpu.SMEM)] + [vmem] * 5 + [anywhere] * 2,
-        out_specs=[anywhere] * 4 + [vmem] * 11 + [anywhere] * 3,
+        out_specs=[anywhere] * 7 + [vmem] * 8 + [anywhere] * 3,
         out_shape=[
             shape((2, units, UNIT, 3 * LANES), BF16),
             shape((model, 2 * own_rows), BF16),
             shape((3 * LANES, model), BF16),
             shape((3 * LANES, model), BF16),
-            shape((2, units, 8, UNIT), F32),
             shape((2, units, BASIS, LANES), BF16),
-            shape((2, units, 8, LANES), F32),
             shape((2, units, BASIS, LANES), BF16),
             shape((2, BASIS, LANES), F32),
+            shape((2, units, 8, UNIT), F32),
+            shape((2, units, 8, LANES), F32),
             shape((2, 32, BASIS), F32),
         ] + [shape((own_rows, width), BF16)] * 4 + [
             shape((4, 8, hidden_part), F32),
@@ -509,9 +511,12 @@
             pltpu.VMEM((2, units, width, UNIT), F32),
             pltpu.VMEM((2, units, UNIT, width), BF16),
             pltpu.VMEM((2, units // 2, UNIT, width), BF16),
+            pltpu.VMEM((2, units, BASIS, LANES), BF16),
+            pltpu.VMEM((2, units, BASIS, LANES), BF16),
+            pltpu.VMEM((2, BASIS, LANES), F32),
             pltpu.SemaphoreType.DMA((hops,)),
             pltpu.SemaphoreType.DMA((hops,)),
-            pltpu.SemaphoreType.DMA((4,)),
+            pltpu.SemaphoreType.DMA((7,)),
         ],
         compiler_params=pltpu.CompilerParams(
             collective_id=1, has_side_effects=True, vmem_limit_bytes=60 << 20
@@ -529,12 +534,11 @@
     grad_in[...] = given_in[...].astype(F32)
     grad_out[...] = given_out[...].astype(F32)
     width = grad_qkv.shape[1]
-    turned = given_qkv[...].astype(F32).T
     for i in range(3):
 
         @pl.when(step == i)
         def _():
-            grad_qkv[0] = turned[i * width : (i + 1) * width]
+            grad_qkv[0] = given_qkv[:, i * width : (i + 1) * width].astype(F32).T
 
     @pl.when(step == 0)
     def _():
@@ -722,9 +726,10 @@
 
 
 def backward_kernel(
-    heads, seg_lengths, qkv, gm_0, gm_1, gm_2, gm_3, logsum, values, probes, key_states, key_end, rows, table,
+    heads, seg_lengths, qkv, gm_0, gm_1, gm_2, gm_3, logsum, values, probes, key_states_in, key_end_in, rows_in, table_in,
     grad_in, grad_out, grad_weight, out, probe_grad, slice_in, slice_out, slice_weight,
     given, query_grad, memory_grad, row_grad, value_carried, value_back, value_in, row_back, row_in, carried, spread, key_grad, value_grad, cols, keys, vals,
+    key_states, key_end, rows, table,
     keep_in, keep_out, keep_weight, core_in, core_out, core_weight, one_in, one_out, one_weight,
     two_in, two_out, two_weight, z_in, z_out, z_weight, send, recv, local_sems,
 ):
@@ -746,6 +751,9 @@
         started.append(hops.start(*args))
         return started[-1]
 
+    tables = set_out(
+        [(key_states_in, key_states), (key_end_in, key_end), (rows_in, rows), (table_in, table)], local_sems, 12
+    )
     given_copies = [go(gm_1, given.at[0, half:], "head", 1), go(gm_3, given.at[1, half:], "head", 1)]
     sums = (
         (grad_in, keep_in, core_in, one_in, two_in, z_in, True),
@@ -964,6 +972,8 @@
     first_hop(0)
     both(read_back, 3)
     second_hop(2)
+    for copy in tables:
+        copy.wait()
     back_copies = []
     for k in range(2):
         gather_back(k, 0)
@@ -1006,7 +1016,7 @@
     hops = 2 + 3 * 4 * 3 + 3 * 3 + 4
     return pl.pallas_call(
         functools.partial(backward_kernel, heads),
-        in_specs=[pl.BlockSpec(memory_space=pltpu.SMEM)] + [vmem] * 12 + [anywhere] * 3,
+        in_specs=[pl.BlockSpec(memory_space=pltpu.SMEM)] + [vmem] * 8 + [anywhere] * 7,
         out_specs=[vmem] * 5,
         out_shape=[shape(qkv.shape, BF16), shape((2, 8, BASIS), F32)] + [shape(part, BF16) for part in slices],
         scratch_shapes=[
@@ -1026,6 +1036,10 @@
             pltpu.VMEM((2, LANES, units * UNIT), BF16),
             pltpu.VMEM((2, units * UNIT, LANES), BF16),
             pltpu.VMEM((2, units * UNIT, LANES), BF16),
+            pltpu.VMEM(key_states.shape, BF16),
+            pltpu.VMEM(key_end.shape, F32),
+            pltpu.VMEM(rows.shape, F32),
+            pltpu.VMEM(table.shape, BF16),
         ]
         + [pltpu.VMEM((4, 2, 2) + part, BF16) for part in slices]
         + [pltpu.VMEM((4, 2, 2) + part, BF16) for part in slices]
@@ -1035,7 +1049,7 @@
         + [
             pltpu.SemaphoreType.DMA((hops,)),
             pltpu.SemaphoreType.DMA((hops,)),
-            pltpu.SemaphoreType.DMA((12,)),
+            pltpu.SemaphoreType.DMA((16,)),
         ],
         compiler_params=pltpu.CompilerParams(
             collective_id=2, has_side_effects=True, vmem_limit_bytes=62 << 20
@@ -1047,13 +1061,17 @@
 
 
 def tail_kernel(
-    heads, outer, grads, first_cols, flat_a, flat_b, grad_residual, source, packed, slice_in, slice_out, slice_weight,
-    sums, in_bias_part, probe_grad, input_grad, whole_in, whole_out, whole_weight, whole_qkv, shared_out, owned_out,
+    heads, outer, grads, flat_a, flat_b, packed, slice_in, slice_out, slice_weight, sums, in_bias_part, probe_grad,
+    first_cols_in, grad_residual_in, source_in, input_grad, whole_in, whole_out, whole_weight, whole_qkv, shared_out, owned_out,
     row_grad, near, kept, part_a, part_b, core_a, core_b, one_a, one_b, two_a, two_b, far_b, total, outer_in,
     gather_in, gather_out, gather_weight, gather_qkv,
-    shared, shared_in, block, block_in, bias_block, bias_in, joined, joined_in, send, recv,
+    shared, shared_in, block, block_in, bias_block, bias_in, joined, joined_in, first_cols, grad_residual, source,
+    send, recv, local_sems,
 ):
     own_rows, model = source.shape
+    loads = set_out(
+        [(first_cols_in, first_cols), (grad_residual_in, grad_residual), (source_in, source)], local_sems, 0
+    )
     units = grads.shape[1]
     half = units // 2
     width = heads * HEAD_DIM
@@ -1095,6 +1113,7 @@
         part = gather.at[:, :, c]
         return go(part, part, "dp", 1)
 
+    loads[0].wait()
     core_copies = []
     for k, part, core in ((1, part_b, core_b), (0, part_a, core_a)):
         product = dot(first_cols[...], grads[k].reshape(2 * own_rows, 3 * LANES))
@@ -1124,6 +1143,8 @@
     block_copy = go(block.at[1], block_in, "head", 2)
     bias_copies = [go(bias_block.at[0], bias_in.at[0], "head", 1), go(bias_block.at[1], bias_in.at[1], "head", 3)]
 
+    loads[1].wait()
+    loads[2].wait()
     value = source[...].astype(F32)
     centred = value - jnp.mean(value, axis=-1, keepdims=True)
     factor = lax.rsqrt(jnp.mean(centred * centred, axis=-1, keepdims=True) + EPSILON)
@@ -1214,7 +1235,7 @@
     hops = units // 2 + 9 + 2 + 2 + 2 + 1 + 5 + 1 + 2 + 3 + 3 + 2 * len(outer)
     return pl.pallas_call(
         functools.partial(tail_kernel, heads, outer),
-        in_specs=[vmem] * 13,
+        in_specs=[vmem] * 10 + [pl.BlockSpec(memory_space=pl.ANY)] * 3,
         out_specs=[vmem] * 7,
         out_shape=[
             shape(source.shape, BF16), shape(plane(slice_in.shape), BF16), shape(plane(slice_out.shape), BF16),
@@ -1248,16 +1269,20 @@
             pltpu.VMEM((2, 8, model), F32),
             pltpu.VMEM((4 + len(outer), 24, model), F32),
             pltpu.VMEM((3 + len(outer), 24, model), F32),
+            pltpu.VMEM(first_cols.shape, BF16),
+            pltpu.VMEM(grad_residual.shape, F32),
+            pltpu.VMEM(source.shape, BF16),
             pltpu.SemaphoreType.DMA((hops,)),
             pltpu.SemaphoreType.DMA((hops,)),
+            pltpu.SemaphoreType.DMA((3,)),
         ],
         compiler_params=pltpu.CompilerParams(
             collective_id=3, has_side_effects=True, vmem_limit_bytes=60 << 20
         ),
         name="tail",
     )(
-        grads, first_cols, flat_a, flat_b, grad_residual, source, packed, slice_in, slice_out, slice_weight, sums,
-        in_bias_part, probe_grad,
+        grads, flat_a, flat_b, packed, slice_in, slice_out, slice_weight, sums, in_bias_part, probe_grad, first_cols,
+        grad_residual, source,
     )
 
 
@@ -1292,7 +1317,7 @@
 
     turned_weight = jnp.transpose(qkv_weight, (1, 2, 0)).reshape(3 * width, model)
     (
-        qkv, first_cols, flat_a, flat_b, logsum, values, probes, key_states, key_end, state_rows,
+        qkv, first_cols, flat_a, flat_b, values, key_states, key_end, logsum, probes, state_rows,
         *mixed, in_bias, far_in, far_out, far_weight,
     ) = forward(seg_lengths, inputs, packed, turned_weight, out_weight, ff_in, ff_out, heads)
     flat = lambda array: array.reshape((shards - 1, slices) + array.shape[4:])

time: 271 us -> 266 us (0.982)
  Pallas kernels: 259 us -> 254 us
where the time goes in v3:
time: 266 us; the launch traced here: 263 us
  Pallas kernels  254 us (95%)
  local copies, waits for them, and re-layouts  5.38 us (2%)
    pallas_call x1, Pallas kernels, forward(): pl.pallas_call(functools.partial(forward_kernel, heads), in_specs=[pl.Blo...  95.8 us
    pallas_call x1, Pallas kernels, backward(): pl.pallas_call(functools.partial(backward_kernel, heads), in_specs=[pl.Bl...  74.7 us
    pallas_call x1, Pallas kernels, tail(): pl.pallas_call(functools.partial(tail_kernel, heads, outer), in_specs=[vm...  48.7 us
    pallas_call x1, Pallas kernels, middle(): pl.pallas_call(middle_kernel, grid_spec=pltpu.PrefetchScalarGridSpec(num_...  29.5 us
    pallas_call x1, Pallas kernels, finish(): pl.pallas_call(finish_kernel, grid=(3,), in_specs=[pl.BlockSpec((model //...  5.34 us

profile of v3, /device:TPU:0, one launch (start us, length us, event | category | flops | bytes accessed | tf_op | source)
XLA Modules:
  0.0 262.6 jit_solution(17394925600301294531)
XLA Ops:
  0.6 0.7 pad_bitcast_fusion
  1.3 0.8 convert_add_fusion
  2.2 1.4 pad_add_fusion.packed.vectors
  3.5 95.8 %forward.1 = (bf16[2,4,256,768]{3,2,1,0:T(8,128)(2,1)}, bf16[768,1024]{1,0:T(8,128)(2,1)}, bf16[768,768]{1,0:T(8,128)(2,1)}, bf16[768,768]{1,0:T(8,128)(2,1)}, b...) custom-call(s32[1,8]{1,0:T(1,128)} %seg_lengths.3, ...), custom_call_target="tpu_custom_call" | custom-call | tf_op jit(solution)/shard_map/forward/pallas_call | solution.py:468
  99.3 29.5 %middle.1 = (bf16[512,768]{1,0:T(8,128)(2,1)}, f32[512,768]{1,0:T(8,128)}, bf16[512,192]{1,0:T(8,128)(2,1)}, bf16[512,192]{1,0:T(8,128)(2,1)}, bf16[512,192]{1,0...) custom-call(bf16[512,768]{1,0:T(8,128)(2,1)} %source_in.1, ...), custom_call_target="tpu_custom_call" | custom-call | flops 16307453952 | bytes 31457280 | tf_op jit(solution)/shard_map/middle/pallas_call | solution.py:682
  128.9 74.7 %backward.1 = (bf16[2,4,256,768]{3,2,1,0:T(8,128)(2,1)}, f32[2,8,512]{2,1,0:T(8,128)}, bf16[96,768]{1,0:T(8,128)(2,1)}, bf16[96,768]{1,0:T(8,128)(2,1)}, bf16[32,768]{1,0:T(8,128)(2,1)}) custom-call(s32[1,8]{1,0:T(1,128)} %seg_lengths.3, bf16[2,4,256,768]{3,2,1,0:T(8,128)(2,1)} %get-tuple-element.70.qkv, bf16[2,256,192]{2,1,0:T(8,128)(2,1)} %bitcast.35, ...), custom_call_target="tpu_custom_call" | custom-call | tf_op jit(solution)/shard_map/backward/pallas_call | solution.py:1017
  203.6 48.7 %tail.1 = (bf16[512,768]{1,0:T(8,128)(2,1)}, bf16[2,2,2,96,768]{4,3,2,1,0:T(8,128)(2,1)}, bf16[2,2,2,96,768]{4,3,2,1,0:T(8,128)(2,1)}, bf16[2,2,2,32,768]{4,3,2,...) custom-call(bf16[2,4,256,768]{3,2,1,0:T(8,128)(2,1)} %get-tuple-element.84.grads, ...), custom_call_target="tpu_custom_call" | custom-call | tf_op jit(solution)/shard_map/tail/pallas_call | solution.py:1236
  252.3 0.0 copy-start
  252.3 1.4 fusion
  253.7 1.8 slice_reduce_fusion
  255.5 0.6 reshape_squeeze.3
  256.1 5.3 %finish.1 = (f32[768,768]{1,0:T(8,128)}, f32[768,768]{1,0:T(8,128)}, f32[192,768]{1,0:T(8,128)}, f32[3,192,768]{2,1,0:T(8,128)}) custom-call(bf16[768,768]{1,0:T(8,128)(2,1)} %bitcast.28, bf16[768,768]{1,0:T(8,128)(2,1)} %bitcast.29, bf16[8,32,768]{2,1,0:T(8,128)(2,1)} %bitcast.34, bf16[768,576]{1,0:T(8,128)(2,1)} %bitcast.32), custom_call_target="tpu_custom_call" | custom-call | tf_op jit(solution)/shard_map/finish/pallas_call | solution.py:553
  261.4 0.0 copy-done
  261.4 0.9 copy.37
  (2 shorter events, 0.0 us)
Async XLA Ops:
  252.3 9.2 %copy-start = (bf16[512,768]{1,0:T(8,128)(2,1)S(1)}, bf16[512,768]{1,0:T(8,128)(2,1)}, u32[]{:S(2)}) copy-start(bf16[512,768]{1,0:T(8,128)(2,1)} %get-tuple-element.135) | copy-start | bytes 2359300

commit v4 on v3

--- a/solution.py
+++ b/solution.py
@@ -137,6 +137,11 @@
         self.send, self.recv, self.used = send, recv, 0
 
     def start(self, source, target, axis, bit):
+        copy = self.make(source, target, axis, bit)
+        copy.start()
+        return copy
+
+    def make(self, source, target, axis, bit):
         copy = pltpu.make_async_remote_copy(
             src_ref=source,
             dst_ref=target,
@@ -146,7 +151,6 @@
             device_id_type=MESH,
         )
         self.used += 1
-        copy.start()
         return copy
 
 
@@ -221,12 +225,23 @@
     gathers = ((far_in, 2, 4), (far_weight, 2, 4), (far_out, 4, 2))
     stage = {}
 
+    for r in (1, 2, 3):
+        stage[r] = [
+            hops.make(in_mine, far_in.at[r - 1, y, x, c], "head", r),
+            hops.make(weight_mine, far_weight.at[r - 1, y, x, c], "head", r),
+            hops.make(out_mine, far_out.at[r - 1, y, x, c], "head", r),
+        ]
+        started.extend(stage[r])
+    at_end = (z == 0) | (z == 3)
+
     def send_chunk(r):
-        stage[r] = [
-            go(in_mine, far_in.at[r - 1, y, x, c], "head", r),
-            go(weight_mine, far_weight.at[r - 1, y, x, c], "head", r),
-            go(out_mine, far_out.at[r - 1, y, x, c], "head", r),
-        ]
+        for copy in stage[r]:
+            copy.start()
+
+    def send_early(first):
+        pl.when(at_end)(functools.partial(send_chunk, 2 if first else 3))
+        pl.when(jnp.logical_not(at_end))(functools.partial(send_chunk, 3 if first else 2))
+
 
     def advance(r, step):
         for copy in stage[r]:
@@ -243,8 +258,7 @@
             stage[r].append(go(part, part, "dp", bit))
 
     send_chunk(1)
-    send_chunk(2)
-    send_chunk(3)
+    send_early(True)
     in_bias[0] = bias_row[...]
     bias_copies = [go(bias_row, in_bias.at[r], "head", r) for r in (1, 2, 3)]
 
@@ -274,6 +288,7 @@
         part = slice(k * UNIT, (k + 1) * UNIT)
         first_rows[own_rows + k * UNIT : own_rows + (k + 1) * UNIT] = near[part]
         project(0, half + k, small[0:1])
+    send_early(False)
 
     advance(1, 1)
     first_cols[:, own_rows:] = near[...].astype(F32).T.astype(BF16)
@@ -971,7 +986,6 @@
     first_hop(3)
     first_hop(0)
     both(read_back, 3)
-    second_hop(2)
     for copy in tables:
         copy.wait()
     back_copies = []
@@ -980,12 +994,13 @@
         back_copies += [
             go(value_back.at[k], value_in.at[1 - k], "head", 2), go(row_back.at[k], row_in.at[1 - k], "head", 2)
         ]
+    second_hop(2)
+    both(attend_back, 3)
     second_hop(1)
-    both(attend_back, 3)
     second_hop(3)
-    second_hop(0)
     third_hop(2)
     both(attend_back, 2)
+    second_hop(0)
     third_hop(1)
     third_hop(3)
     both(attend_back, 1)

time: 266 us -> 261 us (0.981)
  Pallas kernels: 254 us -> 249 us
    pallas_call x1, Pallas kernels: 95.8 us -> 91.3 us  [forward(): pl.pallas_call(functools.partial(forward_kernel, heads), in_specs=[pl.Blo...]
where the time goes in v4:
time: 261 us; the launch traced here: 257 us
  Pallas kernels  249 us (95%)
  local copies, waits for them, and re-layouts  5.38 us (2%)
    pallas_call x1, Pallas kernels, forward(): pl.pallas_call(functools.partial(forward_kernel, heads), in_specs=[pl.Blo...  91.3 us
    pallas_call x1, Pallas kernels, backward(): pl.pallas_call(functools.partial(backward_kernel, heads), in_specs=[pl.Bl...  74.2 us
    pallas_call x1, Pallas kernels, tail(): pl.pallas_call(functools.partial(tail_kernel, heads, outer), in_specs=[vm...  48.2 us
    pallas_call x1, Pallas kernels, middle(): pl.pallas_call(middle_kernel, grid_spec=pltpu.PrefetchScalarGridSpec(num_...  29.5 us
    pallas_call x1, Pallas kernels, finish(): pl.pallas_call(finish_kernel, grid=(3,), in_specs=[pl.BlockSpec((model //...  5.34 us

profile of v4, /device:TPU:0, one launch (start us, length us, event | category | flops | bytes accessed | tf_op | source)
XLA Modules:
  0.0 257.0 jit_solution(8431753828394512290)
XLA Ops:
  0.6 0.7 pad_bitcast_fusion
  1.3 0.8 convert_add_fusion
  2.2 1.4 pad_add_fusion.packed.vectors
  3.5 91.3 %forward.1 = (bf16[2,4,256,768]{3,2,1,0:T(8,128)(2,1)}, bf16[768,1024]{1,0:T(8,128)(2,1)}, bf16[768,768]{1,0:T(8,128)(2,1)}, bf16[768,768]{1,0:T(8,128)(2,1)}, b...) custom-call(s32[1,8]{1,0:T(1,128)} %seg_lengths.3, ...), custom_call_target="tpu_custom_call" | custom-call | tf_op jit(solution)/shard_map/forward/pallas_call | solution.py:483
  94.8 29.5 %middle.1 = (bf16[512,768]{1,0:T(8,128)(2,1)}, f32[512,768]{1,0:T(8,128)}, bf16[512,192]{1,0:T(8,128)(2,1)}, bf16[512,192]{1,0:T(8,128)(2,1)}, bf16[512,192]{1,0...) custom-call(bf16[512,768]{1,0:T(8,128)(2,1)} %source_in.1, ...), custom_call_target="tpu_custom_call" | custom-call | flops 16307453952 | bytes 31457280 | tf_op jit(solution)/shard_map/middle/pallas_call | solution.py:697
  124.3 74.2 %backward.1 = (bf16[2,4,256,768]{3,2,1,0:T(8,128)(2,1)}, f32[2,8,512]{2,1,0:T(8,128)}, bf16[96,768]{1,0:T(8,128)(2,1)}, bf16[96,768]{1,0:T(8,128)(2,1)}, bf16[32,768]{1,0:T(8,128)(2,1)}) custom-call(s32[1,8]{1,0:T(1,128)} %seg_lengths.3, bf16[2,4,256,768]{3,2,1,0:T(8,128)(2,1)} %get-tuple-element.70.qkv, bf16[2,256,192]{2,1,0:T(8,128)(2,1)} %bitcast.35, ...), custom_call_target="tpu_custom_call" | custom-call | tf_op jit(solution)/shard_map/backward/pallas_call | solution.py:1032
  198.5 48.2 %tail.1 = (bf16[512,768]{1,0:T(8,128)(2,1)}, bf16[2,2,2,96,768]{4,3,2,1,0:T(8,128)(2,1)}, bf16[2,2,2,96,768]{4,3,2,1,0:T(8,128)(2,1)}, bf16[2,2,2,32,768]{4,3,2,...) custom-call(bf16[2,4,256,768]{3,2,1,0:T(8,128)(2,1)} %get-tuple-element.84.grads, ...), custom_call_target="tpu_custom_call" | custom-call | tf_op jit(solution)/shard_map/tail/pallas_call | solution.py:1251
  246.7 0.0 copy-start
  246.7 1.4 fusion
  248.1 1.8 slice_reduce_fusion
  249.9 0.6 reshape_squeeze.3
  250.5 5.3 %finish.1 = (f32[768,768]{1,0:T(8,128)}, f32[768,768]{1,0:T(8,128)}, f32[192,768]{1,0:T(8,128)}, f32[3,192,768]{2,1,0:T(8,128)}) custom-call(bf16[768,768]{1,0:T(8,128)(2,1)} %bitcast.28, bf16[768,768]{1,0:T(8,128)(2,1)} %bitcast.29, bf16[8,32,768]{2,1,0:T(8,128)(2,1)} %bitcast.34, bf16[768,576]{1,0:T(8,128)(2,1)} %bitcast.32), custom_call_target="tpu_custom_call" | custom-call | tf_op jit(solution)/shard_map/finish/pallas_call | solution.py:568
  255.9 0.0 copy-done
  255.9 0.9 copy.37
  (2 shorter events, 0.0 us)
Async XLA Ops:
  246.7 9.2 %copy-start = (bf16[512,768]{1,0:T(8,128)(2,1)S(1)}, bf16[512,768]{1,0:T(8,128)(2,1)}, u32[]{:S(2)}) copy-start(bf16[512,768]{1,0:T(8,128)(2,1)} %get-tuple-element.135) | copy-start | bytes 2359300

commit v5 on v4

--- a/solution.py
+++ b/solution.py
@@ -1128,6 +1128,8 @@
         part = gather.at[:, :, c]
         return go(part, part, "dp", 1)
 
+    spreads = [spread_first(gather, along_x) for _, gather, along_x in gathers]
+
     loads[0].wait()
     core_copies = []
     for k, part, core in ((1, part_b, core_b), (0, part_a, core_a)):
@@ -1136,7 +1138,6 @@
         for j in range(8):
             part[j // 4, (j // 2) % 2, j % 2] = product[j * rows : (j + 1) * rows]
         core_copies.append(go(part.at[:, :, 1 - c], core, "dp", 1))
-    spreads = [spread_first(gather, along_x) for _, gather, along_x in gathers]
     for k in range(half):
         kept[k] = row_of(k)
 
@@ -1171,6 +1172,7 @@
     one_copy_a.wait_recv()
     one_a[...] = added(core_a[:, x], one_a[...])
     two_copy_a = go(one_a.at[1 - y], two_a, "dp", 4)
+    spreads = [copy.wait_recv() or spread_second(gather, along_x) for copy, (_, gather, along_x) in zip(spreads, gathers)]
     for copy in row_copies:
         copy.wait_recv()
     two_copy_b.wait_recv()
@@ -1189,7 +1191,6 @@
         [jnp.sum(grad * normal, axis=0, keepdims=True), jnp.sum(grad, axis=0, keepdims=True), sums[0:6]], axis=0
     )
     shared_copies = [go(shared, shared_in.at[r - 1], "head", r) for r in (1, 2, 3)]
-    spreads = [copy.wait_recv() or spread_second(gather, along_x) for copy, (_, gather, along_x) in zip(spreads, gathers)]
 
     two_copy_a.wait_recv()
     own_sum = added(one_a[y], two_a[...]).astype(F32)

time: 261 us -> 259 us (level)
  Pallas kernels: 249 us -> 246 us
where the time goes in v5:
time: 259 us; the launch traced here: 254 us
  Pallas kernels  246 us (95%)
  local copies, waits for them, and re-layouts  5.38 us (2%)
    pallas_call x1, Pallas kernels, forward(): pl.pallas_call(functools.partial(forward_kernel, heads), in_specs=[pl.Blo...  91.3 us
    pallas_call x1, Pallas kernels, backward(): pl.pallas_call(functools.partial(backward_kernel, heads), in_specs=[pl.Bl...  74.2 us
    pallas_call x1, Pallas kernels, tail(): pl.pallas_call(functools.partial(tail_kernel, heads, outer), in_specs=[vm...  45.6 us
    pallas_call x1, Pallas kernels, middle(): pl.pallas_call(middle_kernel, grid_spec=pltpu.PrefetchScalarGridSpec(num_...  29.5 us
    pallas_call x1, Pallas kernels, finish(): pl.pallas_call(finish_kernel, grid=(3,), in_specs=[pl.BlockSpec((model //...  5.34 us

profile of v5, /device:TPU:0, one launch (start us, length us, event | category | flops | bytes accessed | tf_op | source)
XLA Modules:
  0.0 254.4 jit_solution(17467739961720350320)
XLA Ops:
  0.6 0.7 pad_bitcast_fusion
  1.3 0.8 convert_add_fusion
  2.2 1.4 pad_add_fusion.packed.vectors
  3.5 91.3 %forward.1 = (bf16[2,4,256,768]{3,2,1,0:T(8,128)(2,1)}, bf16[768,1024]{1,0:T(8,128)(2,1)}, bf16[768,768]{1,0:T(8,128)(2,1)}, bf16[768,768]{1,0:T(8,128)(2,1)}, b...) custom-call(s32[1,8]{1,0:T(1,128)} %seg_lengths.3, ...), custom_call_target="tpu_custom_call" | custom-call | tf_op jit(solution)/shard_map/forward/pallas_call | solution.py:483
  94.8 29.5 %middle.1 = (bf16[512,768]{1,0:T(8,128)(2,1)}, f32[512,768]{1,0:T(8,128)}, bf16[512,192]{1,0:T(8,128)(2,1)}, bf16[512,192]{1,0:T(8,128)(2,1)}, bf16[512,192]{1,0...) custom-call(bf16[512,768]{1,0:T(8,128)(2,1)} %source_in.1, ...), custom_call_target="tpu_custom_call" | custom-call | flops 16307453952 | bytes 31457280 | tf_op jit(solution)/shard_map/middle/pallas_call | solution.py:697
  124.3 74.2 %backward.1 = (bf16[2,4,256,768]{3,2,1,0:T(8,128)(2,1)}, f32[2,8,512]{2,1,0:T(8,128)}, bf16[96,768]{1,0:T(8,128)(2,1)}, bf16[96,768]{1,0:T(8,128)(2,1)}, bf16[32,768]{1,0:T(8,128)(2,1)}) custom-call(s32[1,8]{1,0:T(1,128)} %seg_lengths.3, bf16[2,4,256,768]{3,2,1,0:T(8,128)(2,1)} %get-tuple-element.70.qkv, bf16[2,256,192]{2,1,0:T(8,128)(2,1)} %bitcast.35, ...), custom_call_target="tpu_custom_call" | custom-call | tf_op jit(solution)/shard_map/backward/pallas_call | solution.py:1032
  198.5 45.6 %tail.1 = (bf16[512,768]{1,0:T(8,128)(2,1)}, bf16[2,2,2,96,768]{4,3,2,1,0:T(8,128)(2,1)}, bf16[2,2,2,96,768]{4,3,2,1,0:T(8,128)(2,1)}, bf16[2,2,2,32,768]{4,3,2,...) custom-call(bf16[2,4,256,768]{3,2,1,0:T(8,128)(2,1)} %get-tuple-element.84.grads, ...), custom_call_target="tpu_custom_call" | custom-call | tf_op jit(solution)/shard_map/tail/pallas_call | solution.py:1252
  244.1 0.0 copy-start
  244.1 1.4 fusion
  245.6 1.8 slice_reduce_fusion
  247.3 0.6 reshape_squeeze.3
  247.9 5.3 %finish.1 = (f32[768,768]{1,0:T(8,128)}, f32[768,768]{1,0:T(8,128)}, f32[192,768]{1,0:T(8,128)}, f32[3,192,768]{2,1,0:T(8,128)}) custom-call(bf16[768,768]{1,0:T(8,128)(2,1)} %bitcast.28, bf16[768,768]{1,0:T(8,128)(2,1)} %bitcast.29, bf16[8,32,768]{2,1,0:T(8,128)(2,1)} %bitcast.34, bf16[768,576]{1,0:T(8,128)(2,1)} %bitcast.32), custom_call_target="tpu_custom_call" | custom-call | tf_op jit(solution)/shard_map/finish/pallas_call | solution.py:568
  253.3 0.0 copy-done
  253.3 0.9 copy.37
  (2 shorter events, 0.0 us)
Async XLA Ops:
  244.1 9.2 %copy-start = (bf16[512,768]{1,0:T(8,128)(2,1)S(1)}, bf16[512,768]{1,0:T(8,128)(2,1)}, u32[]{:S(2)}) copy-start(bf16[512,768]{1,0:T(8,128)(2,1)} %get-tuple-element.135) | copy-start | bytes 2359300

commit v6 on v5

--- a/solution.py
+++ b/solution.py
@@ -1228,13 +1228,16 @@
     last = joined[3 + len(outer)]
     shared_out[...] = last[0:8]
     owned_out[...] = last[8:24]
+    saves = []
     for copy, (_, gather, _), out in zip(spreads, gathers, (whole_in, whole_weight, whole_out)):
         copy.wait_recv()
-        out[...] = gather[...]
+        saves += set_out([(gather, out)], local_sems, 3 + len(saves))
     for copy in qkv_copies:
         copy.wait_recv()
     spread_third(gather_qkv).wait_recv()
-    whole_qkv[...] = gather_qkv[...]
+    saves += set_out([(gather_qkv, whole_qkv)], local_sems, 6)
+    for copy in saves:
+        copy.wait()
     for copy in started:
         copy.wait_send()
 
@@ -1252,7 +1255,7 @@
     return pl.pallas_call(
         functools.partial(tail_kernel, heads, outer),
         in_specs=[vmem] * 10 + [pl.BlockSpec(memory_space=pl.ANY)] * 3,
-        out_specs=[vmem] * 7,
+        out_specs=[vmem] + [pl.BlockSpec(memory_space=pl.ANY)] * 4 + [vmem] * 2,
         out_shape=[
             shape(source.shape, BF16), shape(plane(slice_in.shape), BF16), shape(plane(slice_out.shape), BF16),
             shape(plane(slice_weight.shape), BF16), shape(plane(part), BF16), shape((8, model), F32),
@@ -1290,7 +1293,7 @@
             pltpu.VMEM(source.shape, BF16),
             pltpu.SemaphoreType.DMA((hops,)),
             pltpu.SemaphoreType.DMA((hops,)),
-            pltpu.SemaphoreType.DMA((3,)),
+            pltpu.SemaphoreType.DMA((7,)),
         ],
         compiler_params=pltpu.CompilerParams(
             collective_id=3, has_side_effects=True, vmem_limit_bytes=60 << 20

time: 259 us -> 258 us (level)
  no operation moved by 1% of the time
where the time goes in v6:
time: 258 us; the launch traced here: 254 us
  Pallas kernels  245 us (95%)
  local copies, waits for them, and re-layouts  5.38 us (2%)
    pallas_call x1, Pallas kernels, forward(): pl.pallas_call(functools.partial(forward_kernel, heads), in_specs=[pl.Blo...  91.3 us
    pallas_call x1, Pallas kernels, backward(): pl.pallas_call(functools.partial(backward_kernel, heads), in_specs=[pl.Bl...  74.2 us
    pallas_call x1, Pallas kernels, tail(): pl.pallas_call(functools.partial(tail_kernel, heads, outer), in_specs=[vm...  45 us
    pallas_call x1, Pallas kernels, middle(): pl.pallas_call(middle_kernel, grid_spec=pltpu.PrefetchScalarGridSpec(num_...  29.5 us
    pallas_call x1, Pallas kernels, finish(): pl.pallas_call(finish_kernel, grid=(3,), in_specs=[pl.BlockSpec((model //...  5.34 us

profile of v6, /device:TPU:0, one launch (start us, length us, event | category | flops | bytes accessed | tf_op | source)
XLA Modules:
  0.0 253.8 jit_solution(15826904611973822754)
XLA Ops:
  0.6 0.7 pad_bitcast_fusion
  1.3 0.8 convert_add_fusion
  2.2 1.4 pad_add_fusion.packed.vectors
  3.5 91.3 %forward.1 = (bf16[2,4,256,768]{3,2,1,0:T(8,128)(2,1)}, bf16[768,1024]{1,0:T(8,128)(2,1)}, bf16[768,768]{1,0:T(8,128)(2,1)}, bf16[768,768]{1,0:T(8,128)(2,1)}, b...) custom-call(s32[1,8]{1,0:T(1,128)} %seg_lengths.3, ...), custom_call_target="tpu_custom_call" | custom-call | tf_op jit(solution)/shard_map/forward/pallas_call | solution.py:483
  94.8 29.5 %middle.1 = (bf16[512,768]{1,0:T(8,128)(2,1)}, f32[512,768]{1,0:T(8,128)}, bf16[512,192]{1,0:T(8,128)(2,1)}, bf16[512,192]{1,0:T(8,128)(2,1)}, bf16[512,192]{1,0...) custom-call(bf16[512,768]{1,0:T(8,128)(2,1)} %source_in.1, ...), custom_call_target="tpu_custom_call" | custom-call | flops 16307453952 | bytes 31457280 | tf_op jit(solution)/shard_map/middle/pallas_call | solution.py:697
  124.3 74.2 %backward.1 = (bf16[2,4,256,768]{3,2,1,0:T(8,128)(2,1)}, f32[2,8,512]{2,1,0:T(8,128)}, bf16[96,768]{1,0:T(8,128)(2,1)}, bf16[96,768]{1,0:T(8,128)(2,1)}, bf16[32,768]{1,0:T(8,128)(2,1)}) custom-call(s32[1,8]{1,0:T(1,128)} %seg_lengths.3, bf16[2,4,256,768]{3,2,1,0:T(8,128)(2,1)} %get-tuple-element.70.qkv, bf16[2,256,192]{2,1,0:T(8,128)(2,1)} %bitcast.35, ...), custom_call_target="tpu_custom_call" | custom-call | tf_op jit(solution)/shard_map/backward/pallas_call | solution.py:1032
  198.5 45.0 %tail.1 = (bf16[512,768]{1,0:T(8,128)(2,1)}, bf16[2,2,2,96,768]{4,3,2,1,0:T(8,128)(2,1)}, bf16[2,2,2,96,768]{4,3,2,1,0:T(8,128)(2,1)}, bf16[2,2,2,32,768]{4,3,2,...) custom-call(bf16[2,4,256,768]{3,2,1,0:T(8,128)(2,1)} %get-tuple-element.84.grads, ...), custom_call_target="tpu_custom_call" | custom-call | tf_op jit(solution)/shard_map/tail/pallas_call | solution.py:1255
  243.5 0.0 copy-start
  243.5 1.4 fusion
  244.9 1.8 slice_reduce_fusion
  246.7 0.6 reshape_squeeze.3
  247.3 5.3 %finish.1 = (f32[768,768]{1,0:T(8,128)}, f32[768,768]{1,0:T(8,128)}, f32[192,768]{1,0:T(8,128)}, f32[3,192,768]{2,1,0:T(8,128)}) custom-call(bf16[768,768]{1,0:T(8,128)(2,1)} %bitcast.28, bf16[768,768]{1,0:T(8,128)(2,1)} %bitcast.29, bf16[8,32,768]{2,1,0:T(8,128)(2,1)} %bitcast.34, bf16[768,576]{1,0:T(8,128)(2,1)} %bitcast.32), custom_call_target="tpu_custom_call" | custom-call | tf_op jit(solution)/shard_map/finish/pallas_call | solution.py:568
  252.6 0.0 copy-done
  252.6 0.9 copy.37
  (2 shorter events, 0.0 us)
Async XLA Ops:
  243.5 9.2 %copy-start = (bf16[512,768]{1,0:T(8,128)(2,1)S(1)}, bf16[512,768]{1,0:T(8,128)(2,1)}, u32[]{:S(2)}) copy-start(bf16[512,768]{1,0:T(8,128)(2,1)} %get-tuple-element.135) | copy-start | bytes 2359300
